TPU v7x, 32 devices: a whole 2x2x4 slice. The times are simulated.
32 devices in a mesh: ctx: 4 (over z), fsdp: 8 (over y, x, core).
Axes of the slice: x: 2, y: 2, z: 4, core: 2. Of those that a mesh axis runs over, the one named last changes fastest.
Arguments:
- queries: bfloat16 [8, 1024, 2048], P('fsdp', 'ctx'), may hold values from -36 to 36
- keys: bfloat16 [8, 1024, 512], P('fsdp', 'ctx'), may hold values from -6 to 6
- values: bfloat16 [8, 1024, 512], P('fsdp', 'ctx'), may hold values from -6 to 6
- resid: bfloat16 [8, 1024, 2048], P('fsdp', 'ctx'), may hold values from -6 to 6
- grad_out: bfloat16 [8, 1024, 2048], P('fsdp', 'ctx'), may hold values from -8 to 8
- w_out: bfloat16 [2048, 2048], P(None, 'fsdp'), may hold values from -0.125 to 0.125
- block_list: int32 [8, 8], P('ctx'), may hold values from 0 to 7, as said below
- block_count: int32 [8], P('ctx'), may hold values from 1 to 8, as said below
Outputs:
- mixed: bfloat16 [8, 1024, 2048], P('fsdp', 'ctx')
- query_grad: bfloat16 [8, 1024, 2048], P('fsdp', 'ctx')
- key_grad: bfloat16 [8, 1024, 512], P('fsdp', 'ctx')
- value_grad: bfloat16 [8, 1024, 512], P('fsdp', 'ctx')
- proj_grad: float32 [2048, 2048], P('ctx', 'fsdp')
Inputs may be any that keep to these rules, and one draw needn't show every extreme that they name: `block_list`: row r lists the key blocks of query block r within its sequence: entry 0 is r itself; entries 1 to block_count[r] - 1 are distinct blocks before r; entries from block_count[r] on are ignored and hold r or earlier blocks. block_count[r] is at most min(r + 1, 8); the last query block has exactly 8.
All inputs are finite; a program needn't handle non-finite values.
Results may differ from a plain program's by a relative error of at most 0.025.
Values may be sent and summed in bfloat16 or wider, within the bound.
No kernel may reach another device: no remote copies, remote signals or barrier semaphores. Data moves between devices by JAX's collectives and lax.ppermute only.
A program may use at most 192 MiB of HBM per device.

v0:
```python
import functools
import math

import jax
import jax.numpy as jnp
from jax import lax
from jax.experimental import pallas as pl
from jax.experimental.pallas import tpu as pltpu
from jax.sharding import PartitionSpec as P

QUERY_HEADS = 16
KEY_VALUE_HEADS = 4
HEAD_DIM = 128
BLOCK_SIZE = 128
KEY_SLOTS = 8

GROUP = QUERY_HEADS // KEY_VALUE_HEADS
CORE_KV = KEY_VALUE_HEADS // 2
HALF = QUERY_HEADS * HEAD_DIM // 2
KV_HALF = CORE_KV * HEAD_DIM
STACK = GROUP * BLOCK_SIZE
WIDE = GROUP * HEAD_DIM
SCALE = 1.0 / math.sqrt(HEAD_DIM)
EXP2_SCALE = SCALE * math.log2(math.e)
NEG = -1e30
F32 = jnp.float32
BF16 = jnp.bfloat16
VMEM_LIMIT = 56 * 1024 * 1024
NT = (((1,), (1,)), ((), ()))


def dot(a, b):
    return jnp.dot(a, b, preferred_element_type=F32)


def stack_heads(x):
    return jnp.concatenate([x[:, h * HEAD_DIM:(h + 1) * HEAD_DIM] for h in range(GROUP)], axis=0)


def cost(weight):
    return pl.CostEstimate(flops=int(weight * 1e9), bytes_accessed=1_000_000, transcendentals=0)


def params(steps):
    return pltpu.CompilerParams(dimension_semantics=("arbitrary",) * steps, vmem_limit_bytes=VMEM_LIMIT)


def fill_kv(kv_refs, kv_sc, rows, nc):
    for n, ref in enumerate(kv_refs):
        d = n % nc
        for u in range(2 * CORE_KV):
            kv_sc[n // nc, u, d * rows:(d + 1) * rows, :] = ref[:, u * HEAD_DIM:(u + 1) * HEAD_DIM]


def slot_rows(bl_ref, c, i, j, nb):
    b = bl_ref[i, j]
    chip = b // nb
    return pl.multiple_of(((c - chip) * nb + (b - chip * nb)) * BLOCK_SIZE, BLOCK_SIZE)


def masked_scores(k_cat, qs, slots, count):
    s_t = lax.dot_general(k_cat, qs, NT, preferred_element_type=F32)
    key = lax.broadcasted_iota(jnp.int32, (BLOCK_SIZE, STACK), 0)
    query = lax.broadcasted_iota(jnp.int32, (BLOCK_SIZE, STACK), 1) & (BLOCK_SIZE - 1)
    parts = [jnp.where(key <= query, s_t[:BLOCK_SIZE], NEG)]
    for j in range(1, slots):
        parts.append(jnp.where(j < count, s_t[j * BLOCK_SIZE:(j + 1) * BLOCK_SIZE], NEG))
    return jnp.concatenate(parts, axis=0)


def by_count(count, run):
    small = KEY_SLOTS // 2

    @pl.when(count <= small)
    def _():
        run(small)

    @pl.when(count > small)
    def _():
        run(KEY_SLOTS)


def wide_part(ref, g):
    return stack_heads(ref[0, :, g * WIDE:(g + 1) * WIDE])


def slot_cat(kv_sc, s, u, starts):
    return jnp.concatenate([kv_sc[s, u, pl.ds(at, BLOCK_SIZE), :] for at in starts], axis=0)


def forward_kernel(nc, nb, bl_ref, bc_ref, meta_ref, q_ref, *rest):
    kv_refs, (a_ref, *at_refs, st_ref, kv_sc) = rest[:2 * nc], rest[2 * nc:]
    step = pl.program_id(0)
    s, i = step // nb, step % nb

    @pl.when(step == 0)
    def _():
        fill_kv(kv_refs, kv_sc, nb * BLOCK_SIZE, nc)

    c = meta_ref[0]
    count = bc_ref[i]

    def run(slots):
        starts = [slot_rows(bl_ref, c, i, j, nb) for j in range(slots)]
        for g in range(CORE_KV):
            qs = wide_part(q_ref, g)
            k_cat = slot_cat(kv_sc, s, g, starts)
            v_cat = slot_cat(kv_sc, s, CORE_KV + g, starts)
            s_t = masked_scores(k_cat, qs, slots, count)
            top = jnp.max(s_t, axis=0, keepdims=True)
            p = jnp.exp2((s_t - top) * EXP2_SCALE)
            total = jnp.sum(p, axis=0, keepdims=True)
            a_t = dot(v_cat.T, p.astype(BF16)) / total
            st_ref[0, g] = top * EXP2_SCALE + jnp.log2(total)
            for h in range(GROUP):
                part = a_t[:, h * BLOCK_SIZE:(h + 1) * BLOCK_SIZE]
                at_refs[g][0, h * HEAD_DIM:(h + 1) * HEAD_DIM, :] = part.astype(BF16)
                lane = g * WIDE + h * HEAD_DIM
                a_ref[0, :, lane:lane + HEAD_DIM] = part.T.astype(BF16)

    by_count(count, run)


def kv_specs(nc, rows):
    return [pl.BlockSpec((rows, 2 * KV_HALF), lambda n, *_: (0, 0)) for _ in range(2 * nc)]


def forward(bl, bc, meta, q, kvs, weight=20):
    nc, rows = len(kvs) // 2, q.shape[1]
    nb = rows // BLOCK_SIZE
    wide = pl.BlockSpec((1, BLOCK_SIZE, HALF), lambda n, *_: (n // nb, n % nb, 0))
    turned = pl.BlockSpec((1, WIDE, BLOCK_SIZE), lambda n, *_: (n // nb, 0, n % nb))
    return pl.pallas_call(
        functools.partial(forward_kernel, nc, nb),
        grid_spec=pltpu.PrefetchScalarGridSpec(
            num_scalar_prefetch=3,
            grid=(2 * nb,),
            in_specs=[wide, *kv_specs(nc, rows)],
            out_specs=[wide, *[turned] * CORE_KV, pl.BlockSpec((1, CORE_KV, 1, STACK), lambda n, *_: (n, 0, 0, 0))],
            scratch_shapes=[pltpu.VMEM((2, 2 * CORE_KV, nc * rows, HEAD_DIM), BF16)],
        ),
        out_shape=[
            jax.ShapeDtypeStruct((2, rows, HALF), BF16),
            *[jax.ShapeDtypeStruct((2, WIDE, rows), BF16)] * CORE_KV,
            jax.ShapeDtypeStruct((2 * nb, CORE_KV, 1, STACK), F32),
        ],
        compiler_params=params(1),
        cost_estimate=cost(weight),
        name="attention_forward",
    )(bl, bc, meta, q, *kvs)


def backward_kernel(nc, nb, plan, width, bl_ref, bc_ref, meta_ref, q_ref, a_ref, st_ref, *rest):
    kv_refs, rest = rest[:nc], rest[nc:]
    if plan:
        (g0_ref, g1_ref, *w_refs), (dq_ref, dkv_ref, spare_ref, kv_sc, acc, do_ref) = rest[:-6], rest[-6:]
    else:
        do_ref, dq_ref, dkv_ref, kv_sc, acc = rest
    i = pl.program_id(0)
    rows = nb * BLOCK_SIZE

    @pl.when(i == 0)
    def _():
        if plan:
            for span, part in output_grad_product(plan, width, meta_ref, (g0_ref, g1_ref), w_refs):
                spare_ref[:, span] = part[:rows].astype(BF16)
                do_ref[:, span] = part[rows:].astype(BF16)
        fill_kv(kv_refs, kv_sc, rows, nc)
        acc[...] = jnp.zeros_like(acc)

    c = meta_ref[0]
    count = bc_ref[i]

    def run(slots):
        starts = [slot_rows(bl_ref, c, i, j, nb) for j in range(slots)]
        here = pl.ds(pl.multiple_of(i * BLOCK_SIZE, BLOCK_SIZE), BLOCK_SIZE)
        for g in range(CORE_KV):
            qs = wide_part(q_ref, g)
            dos = stack_heads(do_ref[here, g * WIDE:(g + 1) * WIDE])
            outs = wide_part(a_ref, g)
            row_dot = jnp.sum((dos.astype(F32) * outs.astype(F32)).T, axis=0, keepdims=True)
            k_cat = slot_cat(kv_sc, 0, g, starts)
            v_cat = slot_cat(kv_sc, 0, CORE_KV + g, starts)
            s_t = masked_scores(k_cat, qs, slots, count)
            p = jnp.exp2(s_t * EXP2_SCALE - st_ref[0, g])
            dp = lax.dot_general(v_cat, dos, NT, preferred_element_type=F32)
            ds = (p * (dp - row_dot)).astype(BF16)
            dv = dot(p.astype(BF16), dos)
            dk = dot(ds, qs) * SCALE
            dq_t = dot(k_cat.T, ds) * SCALE
            for h in range(GROUP):
                part = dq_t[:, h * BLOCK_SIZE:(h + 1) * BLOCK_SIZE]
                lane = g * WIDE + h * HEAD_DIM
                dq_ref[:, lane:lane + HEAD_DIM] = part.T.astype(BF16)
            lanes = slice(g * HEAD_DIM, (g + 1) * HEAD_DIM)
            for j in range(slots):
                at = pl.ds(pl.multiple_of(bl_ref[i, j] * BLOCK_SIZE, BLOCK_SIZE), BLOCK_SIZE)
                acc[0, at, lanes] += dk[j * BLOCK_SIZE:(j + 1) * BLOCK_SIZE]
                acc[1, at, lanes] += dv[j * BLOCK_SIZE:(j + 1) * BLOCK_SIZE]

    by_count(count, run)

    @pl.when(i == nb - 1)
    def _():
        dkv_ref[...] = acc[...].astype(BF16)


def backward(bl, bc, meta, s, q, a, st, kvs, extra, plan=(), weight=20):
    nc, rows = len(kvs), q.shape[1]
    nb, width = rows // BLOCK_SIZE, extra[-1].shape[-1]
    wide = pl.BlockSpec((1, BLOCK_SIZE, HALF), lambda n, *_: (s, n, 0))
    whole = pl.BlockSpec(memory_space=pltpu.VMEM)
    grad = jax.ShapeDtypeStruct((rows, HALF), BF16)
    return pl.pallas_call(
        functools.partial(backward_kernel, nc, nb, plan, width),
        grid_spec=pltpu.PrefetchScalarGridSpec(
            num_scalar_prefetch=3,
            grid=(nb,),
            in_specs=[
                wide,
                wide,
                pl.BlockSpec((1, CORE_KV, 1, STACK), lambda n, *_: (s * nb + n, 0, 0, 0)),
                *[whole] * (nc + len(extra)),
            ],
            out_specs=[
                pl.BlockSpec((BLOCK_SIZE, HALF), lambda n, *_: (n, 0)),
                pl.BlockSpec((2, nc * rows, KV_HALF), lambda n, *_: (0, 0, 0)),
                *[pl.BlockSpec((rows, HALF), lambda n, *_: (0, 0))] * bool(plan),
            ],
            scratch_shapes=[
                pltpu.VMEM((1, 2 * CORE_KV, nc * rows, HEAD_DIM), BF16),
                pltpu.VMEM((2, nc * rows, KV_HALF), F32),
                *[pltpu.VMEM((rows, HALF), BF16)] * bool(plan),
            ],
        ),
        out_shape=[grad, jax.ShapeDtypeStruct((2, nc * rows, KV_HALF), BF16), *[grad] * bool(plan)],
        compiler_params=params(1),
        cost_estimate=cost(weight),
        name="attention_backward",
    )(bl, bc, meta, q, a, st, *kvs, *extra)


def column(meta_ref, chip, core, width):
    at = ((meta_ref[2] ^ chip) * 2 + (meta_ref[1] ^ core)) * width
    return pl.ds(pl.multiple_of(at, width), width)


def read_piece(w_refs, piece):
    ref, lead, start = piece
    rows = pl.ds(start, HALF // 2)
    return w_refs[ref][rows, :] if lead is None else w_refs[ref][lead, rows, :]


def output_grad_product(plan, width, meta_ref, g_refs, w_refs):
    grads = jnp.concatenate(
        [
            jnp.concatenate([ref[:, column(meta_ref, chip, core, width)] for ref in g_refs], axis=0)
            for chip, core, _ in plan
        ],
        axis=1,
    )
    for r in range(2):
        w = jnp.concatenate([read_piece(w_refs, pieces[r]) for _, _, pieces in plan], axis=1)
        yield slice(r * (HALF // 2), (r + 1) * (HALF // 2)), lax.dot_general(
            grads, w, NT, preferred_element_type=F32
        )


def mix_kernel(plan, width, meta_ref, a_ref, resid_ref, *rest):
    w_refs, (own_ref, other_ref) = rest[:-2], rest[-2:]
    rows = resid_ref.shape[0]
    a = jnp.concatenate([a_ref[0], a_ref[1]], axis=0)
    for chip, core, pieces in plan:
        at = column(meta_ref, chip, core, width)
        part = dot(a, jnp.concatenate([read_piece(w_refs, piece) for piece in pieces], axis=0))
        own_ref[:, at] = part[:rows] + resid_ref[:, at].astype(F32)
        other_ref[:, at] = part[rows:].astype(BF16)


def mix(meta, a, resid, plan, arrays, weight=20):
    width = arrays[0].shape[-1]
    whole = pl.BlockSpec(memory_space=pltpu.VMEM)
    return pl.pallas_call(
        functools.partial(mix_kernel, plan, width),
        in_specs=[pl.BlockSpec(memory_space=pltpu.SMEM)] + [whole] * (2 + len(arrays)),
        out_specs=[whole, whole],
        out_shape=[jax.ShapeDtypeStruct(resid.shape, F32), jax.ShapeDtypeStruct(resid.shape, BF16)],
        compiler_params=params(0),
        cost_estimate=cost(weight),
        name="mix",
    )(meta, a, resid, *arrays)


def proj_kernel(count, width, cols_ref, g0_ref, g1_ref, *refs):
    inputs, outputs = refs[:8], refs[8:]
    for r in range(2):
        at_ref, far_ref, near0_ref, near1_ref = inputs[4 * r:4 * r + 4]
        lhs = jnp.concatenate([at_ref[0], at_ref[1], far_ref[0], far_ref[1]], axis=1)
        for n in range(count):
            for side in range(2):
                own = pl.ds(pl.multiple_of(cols_ref[r, n, side, 0], width), width)
                near = pl.ds(pl.multiple_of(cols_ref[r, n, side, 1], width), width)
                rhs = [g0_ref[:, own], g1_ref[:, own], near0_ref[:, near], near1_ref[:, near]]
                out = dot(lhs, jnp.concatenate(rhs, axis=0))
                outputs[(r * count + n) * 2 + side][...] = out.astype(BF16)


def proj_parts(cols, g0, g1, inputs, width, weight=20):
    count = cols.shape[1]
    whole = pl.BlockSpec(memory_space=pltpu.VMEM)
    return pl.pallas_call(
        functools.partial(proj_kernel, count, width),
        in_specs=[pl.BlockSpec(memory_space=pltpu.SMEM)] + [whole] * 10,
        out_specs=[whole] * (4 * count),
        out_shape=[jax.ShapeDtypeStruct((WIDE, width), BF16)] * (4 * count),
        compiler_params=params(0),
        cost_estimate=cost(weight),
        name="proj_parts",
    )(cols, g0, g1, *inputs)


def halve_kernel(meta_ref, q0_ref, q1_ref, out_ref):
    out_ref[0] = q0_ref[...]
    out_ref[1] = q1_ref[...]


def halve(meta, q0, q1, weight=20):
    rows = q0.shape[0]
    half = pl.BlockSpec((rows, HALF), lambda n, m: (0, m[1]))
    return pl.pallas_call(
        halve_kernel,
        grid_spec=pltpu.PrefetchScalarGridSpec(
            num_scalar_prefetch=1,
            grid=(1,),
            in_specs=[half, half],
            out_specs=pl.BlockSpec((2, rows, HALF), lambda n, m: (0, 0, 0)),
        ),
        out_shape=jax.ShapeDtypeStruct((2, rows, HALF), BF16),
        compiler_params=params(1),
        cost_estimate=cost(weight),
        name="halve",
    )(meta, q0, q1)


def after(x, *earlier):
    return lax.optimization_barrier((x, *earlier))[0]


def local(nc, nf, queries, keys, values, resid, grad_out, w_out, block_list, block_count):
    chips = nf // 2
    bits = [1 << b for b in range(chips.bit_length() - 1)]
    routes = (bits, bits[::-1])
    mid = HALF // 2
    c = lax.axis_index("ctx")
    f = lax.axis_index("fsdp")
    core, chip = f % 2, f // 2
    meta = jnp.stack([c, core, chip]).astype(jnp.int32)
    rows = queries.shape[1]
    width = w_out.shape[1]

    def to_core(x):
        return lax.ppermute(x, "fsdp", [(p, p ^ 1) for p in range(nf)])

    def to_chip(x, bit):
        return lax.ppermute(x, "fsdp", [(p, p ^ (2 * bit)) for p in range(nf)])

    def place(mine, theirs, axis):
        return jnp.where(
            core == 0,
            jnp.concatenate([mine, theirs], axis=axis),
            jnp.concatenate([theirs, mine], axis=axis),
        )

    def kv_part(which):
        cut = lambda x: lax.dynamic_slice_in_dim(x[0], which * KV_HALF, KV_HALF, 1)
        return jnp.concatenate([cut(keys), cut(values)], axis=1)

    def hop_up(x, step):
        return lax.ppermute(x, "ctx", [(p, p + 1) for p in range(step - 1, nc - 1)])

    q0, g0 = queries[0], grad_out[0]
    w_mine = lax.dynamic_slice_in_dim(w_out, core * HALF, HALF, 0)
    kvs0 = [kv_part(core)]
    kvs1 = [to_core(kv_part(1 - core))]
    w_theirs = to_core(lax.dynamic_slice_in_dim(w_out, (1 - core) * HALF, HALF, 0))

    arrays = [w_mine, w_theirs]
    held = {(0, side, r): (side, None, r * mid) for side in range(2) for r in range(2)}
    last = {}
    for side in range(2):
        for bit in bits:
            got = to_chip(after(arrays[side], *last.get(bit, ())), bit)
            for r in range(2):
                held[bit, side, r] = (len(arrays), None, r * mid)
            arrays.append(got)
            last[bit] = (got,)
    for step in range(1, nc):
        kvs0.append(hop_up(kvs0[-1], step))
        kvs1.append(hop_up(kvs1[-1], step))
    for step in range(1, len(bits)):
        for r in range(2):
            bit = routes[r][step]
            known = [0]
            for earlier in routes[r][:step]:
                known += [rel ^ earlier for rel in known]
            sources = [(rel, side) for rel in known[1:] for side in range(2)]
            parts = []
            for source in sources:
                ref, lead, first = held[(*source, r)]
                x = arrays[ref] if lead is None else arrays[ref][lead]
                parts.append(x[first:first + mid])
            got = to_chip(after(jnp.stack(parts), *last[bit], kvs0[nc - 2], kvs1[nc - 2]), bit)
            for n, (rel, side) in enumerate(sources):
                held[rel ^ bit, side, r] = (len(arrays), n, 0)
            arrays.append(got)
            last[bit] = (got,)
    w_gate = [x for bit in bits for x in last[bit]]
    g1 = to_core(after(g0, w_theirs, kvs1[0]))
    q1 = to_core(after(q0, g1))
    plan = [
        (rel, core_bit, [held[rel, core_bit, r] for r in range(2)]) for rel in range(chips) for core_bit in range(2)
    ]
    with_bit = [[rel for rel in range(chips) if rel & route[0]] for route in routes]
    without = [[rel ^ routes[r][0] for rel in with_bit[r]] for r in range(2)]

    def grad_columns(rels):
        cut = lambda rel: lax.dynamic_slice_in_dim(g0, (chip ^ rel) * 2 * width, 2 * width, 1)
        return jnp.concatenate([cut(rel) for rel in rels], axis=1)

    q_both = halve(meta, after(q0, kvs0[nc - 2], kvs1[nc - 2]), q1)
    kvs0[-1], kvs1[-1] = after(kvs0[-1], q_both), after(kvs1[-1], q_both)
    kvs = kvs0 + kvs1
    a_both, *at, st = forward(block_list, block_count, meta, q_both, kvs)
    near_grads = []
    for r in range(2):
        got = to_chip(after(grad_columns(with_bit[r]), *w_gate, a_both), routes[r][0])
        near_grads.append((got, to_core(got)))
    far_at = [to_chip(after(at[r], near_grads[r][0]), routes[r][0]) for r in range(2)]
    def total(parts):
        return functools.reduce(jnp.add, [x.astype(F32) for x in parts])

    class Chain:
        def __init__(self, shard, sign):
            self.shard, self.sign, self.step = shard, sign, 0

        def send(self):
            self.step += 1
            t = jnp.clip(c - self.sign * (self.step - nc), 0, nc - 1)
            own = self.shard(t)
            self.sent = own if self.step == 1 else total([own, self.got]).astype(BF16)
            reach = [p for p in range(nc) if (nc - 1 - p if self.sign < 0 else p) < self.step]
            pairs = [(p, p + self.sign) for p in reach if 0 <= p + self.sign < nc]
            self.got = lax.ppermute(self.sent, "ctx", pairs)

        def gate(self, *earlier):
            self.got = after(self.got, *earlier)

        def result(self):
            while self.step < nc - 1:
                self.send()
            return self.got

    kv_shard = lambda dkv: lambda t: lax.dynamic_slice_in_dim(dkv, t * rows, rows, 1)
    listed = (block_list, block_count, meta)
    dq1, dkv1, do0 = backward(*listed, 1, q_both, a_both, st, kvs1, (g0, g1, *arrays), plan)

    def hop_down(step, got):
        parts = []
        for lane, dkv in ((0, dkv1), (1, dkv0)):
            hop = step - lane
            if 1 <= hop < nc:
                own = kv_shard(dkv)(jnp.maximum(c + hop - nc, 0))
                parts.append(own if hop == 1 else total([own, got[lane]]).astype(BF16))
            else:
                parts.append(None)
        sending = jnp.stack([x for x in parts if x is not None])
        moved = lax.ppermute(sending, "ctx", [(p, p - 1) for p in range(max(nc - step, 1), nc)])
        return sending, moved

    def unpack(step, moved):
        return (moved[0] if step < nc else None, moved[-1] if step > 1 else None)

    dkv0 = None
    sending, moved = hop_down(1, None)
    dq0, dkv0 = backward(*listed, 0, after(q_both, sending), a_both, st, kvs0, (do0,))
    sending, moved = hop_down(2, unpack(1, after(moved, dkv0)))

    inputs = []
    for r in range(2):
        inputs += [at[r], after(far_at[r], dkv0), *near_grads[r]]
    order = [
        [[jnp.stack([((chip ^ rel) * 2 + (core ^ side)) * width, (n * 2 + (core ^ side)) * width]) for side in range(2)]
         for n, rel in enumerate(without[r])]
        for r in range(2)
    ]
    cols = jnp.stack([jnp.stack([jnp.stack(pair) for pair in route]) for route in order]).astype(jnp.int32)
    parts = proj_parts(after(cols, sending), g0, g1, inputs, width)
    count = len(without[0])
    own_mix, other_mix = mix(meta, after(a_both, parts[0]), resid[0], plan, arrays)
    sending, moved = hop_down(3, unpack(2, after(moved, other_mix)))
    for step in range(4, nc + 1):
        if step == nc:
            sum1 = total([kv_shard(dkv1)(c), moved[0]]).astype(BF16)
        sending_more, moved = hop_down(step, unpack(step - 1, moved))
    sum0 = total([kv_shard(dkv0)(c), moved[-1]]).astype(BF16)
    query_grad = place(dq0, to_core(after(dq1, other_mix)), 1)[None]

    def reduce_chips(r):
        have = {(rel, side): parts[(r * count + n) * 2 + side] for n, rel in enumerate(without[r]) for side in range(2)}
        for bit in routes[r][1:-1]:
            far = sorted({rel for rel, _ in have if rel & bit})
            for side in range(2):
                got = to_chip(jnp.stack([have.pop((rel, side)).astype(BF16) for rel in far]), bit)
                for n, rel in enumerate(far):
                    have[rel ^ bit, side] = total([have[rel ^ bit, side], got[n]])
        bit = routes[r][-1]
        same = to_chip(have[bit, 0].astype(BF16), bit)
        cross = lax.ppermute(have[bit, 1].astype(BF16), "fsdp", [(p, p ^ (2 * bit) ^ 1) for p in range(nf)])
        return have[0, 0], have[0, 1], after(same, other_mix), after(cross, other_mix)

    reduced = [reduce_chips(r) for r in range(2)]
    swapped = to_core(after(jnp.concatenate([part[1].astype(BF16) for part in reduced], axis=0), other_mix))
    mine = [total([near, same]) for near, _, same, _ in reduced]
    theirs = [total([swapped[r * mid:(r + 1) * mid], reduced[r][3]]) for r in range(2)]
    proj_rows = jnp.concatenate(mine + theirs, axis=0).astype(BF16)
    proj_rows = after(proj_rows, sending)
    share = QUERY_HEADS * HEAD_DIM // nc

    def proj_shard(t):
        start = t * share
        return lax.dynamic_slice_in_dim(proj_rows, start + (core * HALF) * jnp.where(start < HALF, 1, -1), share, 0)

    proj_down, proj_up = Chain(proj_shard, -1), Chain(proj_shard, 1)
    for _ in range(nc - 1):
        proj_down.send()
        proj_up.send()
        proj_down.got, proj_up.got = lax.optimization_barrier((proj_down.got, proj_up.got))
    proj_grad = total([proj_shard(c), proj_down.got, proj_up.got])
    mixed = total([own_mix, to_core(other_mix)]).astype(BF16)
    grads = place(sum0, to_core(sum1), 2)
    return mixed[None], query_grad, grads[:1], grads[1:], proj_grad


def solution(mesh):
    rows = P("fsdp", "ctx", None)
    body = functools.partial(local, mesh.shape["ctx"], mesh.shape["fsdp"])
    return jax.shard_map(
        body,
        mesh=mesh,
        in_specs=(rows, rows, rows, rows, rows, P(None, "fsdp"), P("ctx", None), P("ctx")),
        out_specs=(rows, rows, rows, rows, P("ctx", "fsdp")),
        check_vma=False,
    )
```

profile of v0, /device:TPU:0, one launch (start us, length us, event | category | flops | bytes accessed | tf_op | source)
XLA Modules:
  0.0 154.6 jit_solution(8462318588303304668)
XLA Ops:
  0.7 1.4 constant_dynamic-slice_fusion.2
  2.1 3.0 %collective-permute-start.11 = (bf16[1024,256]{1,0:T(8,128)(2,1)S(1)}, bf16[1024,256]{1,0:T(8,128)(2,1)}, u32[]{:S(2)}, u32[]{:S(2)}) collective-permute-start(bf16[1024,256]{1,0:T(8,128)(2,1)S(1)} %get-tuple-element.118.rest_6_.rest_0_), channel_id=1, source_target_pairs={{0,4},{1,5},{2,6},{3,7},{4,0},{5,1},{6,2},{7,3},{8,12},{9,13},{10,... | collective-permute-start | bytes 1572872 | tf_op jit(solution)/shard_map/ppermute | solution.py:365
  5.1 1.5 collective-permute-start.10
  8.0 4.2 %collective-permute-start = (bf16[256,512]{1,0:T(8,128)(2,1)}, bf16[256,512]{1,0:T(8,128)(2,1)}, u32[]{:S(2)}, u32[]{:S(2)}) collective-permute-start(bf16[256,512]{1,0:T(8,128)(2,1)} %pad_maximum_fusion.8.rest_0_), channel_id=1, source_target_pairs={{0,8},{8,16},{16,24},{1,9},{9,17},{17,25},{2,10},{10,18},{18,26},{... | collective-permute-start | bytes 786440 | tf_op jit(solution)/shard_map/ppermute | solution.py:379
  13.5 3.5 %collective-permute-start.3 = (bf16[256,512]{1,0:T(8,128)(2,1)}, bf16[256,512]{1,0:T(8,128)(2,1)}, u32[]{:S(2)}, u32[]{:S(2)}) collective-permute-start(bf16[256,512]{1,0:T(8,128)(2,1)} %copy-done.28), channel_id=1, source_target_pairs={{0,8},{8,16},{16,24},{1,9},{9,17},{17,25},{2,10},{10,18},{18,26},{... | collective-permute-start | bytes 786440 | tf_op jit(solution)/shard_map/ppermute | solution.py:379
  21.0 2.1 %collective-permute-done.3.rest_5_.rest_1_ = bf16[256,512]{1,0:T(8,128)(2,1)} collective-permute-done((bf16[256,512]{1,0:T(8,128)(2,1)}, bf16[256,512]{1,0:T(8,128)(2,1)}, u32[]{:S(2)}, u32[]{:S(2)}) %collective-permute-start.3) | collective-permute-done | bytes 262176 | tf_op jit(solution)/shard_map/ppermute | solution.py:379
  23.9 1.0 slice_bitcast_fusion.3
  25.6 1.0 slice_bitcast_fusion.5
  27.2 4.8 %collective-permute-done.13.rest_11_.rest_5_ = bf16[1024,256]{1,0:T(8,128)(2,1)S(1)} collective-permute-done((bf16[1024,256]{1,0:T(8,128)(2,1)}, bf16[1024,256]{1,0:T(8,128)(2,1)S(1)}, u32[]{:S(2)}, u32[]{:S(2)}) %collective-permute-start.13) | collective-permute-done | bytes 524320 | tf_op jit(solution)/shard_map/ppermute | solution.py:365
  32.9 0.8 collective-permute-start.15
  33.8 1.3 collective-permute-start.14
  35.1 1.0 copy-done.15
  36.1 2.9 %halve.1.q_ref = bf16[2,256,1024]{2,1,0:T(8,128)(2,1)} custom-call(s32[3]{0:T(128)} %pad_add_fusion.3.meta_ref, bf16[256,2048]{1,0:T(8,128)(2,1)} %bitcast.104, bf16[256,2048]{1,0:T(8,128)(2,1)} %copy-done.15), custom_call_target="tpu_custom_call" | custom-call | flops 20000000000 | bytes 1000000 | tf_op jit(solution)/shard_map/halve/pallas_call | solution.py:330
  40.4 8.8 %attention_forward.1 = (bf16[2,256,1024]{2,1,0:T(8,128)(2,1)}, bf16[2,512,256]{2,1,0:T(8,128)(2,1)}, bf16[2,512,256]{2,1,0:T(8,128)(2,1)}, f32[4,2,1,512]{3,2,1,0:T(1,128)}) custom-call(s32[2,8]{1,0:T(2,128)} %bl_ref.5, s32[2]{0:T(128)} %bc_ref.5, s32[3]{0:T(128)} %pad_add_fusion.3.meta_ref, bf16[2,256,1024]{2,1,0:T(8,128)(2,1)} %halve.1.q_ref, ...), custom_call_target="tpu_custom_call" | custom-call | flops 20000000000 | bytes 1000000 | tf_op jit(solution)/shard_map/attention_forward/pallas_call | solution.py:133
  49.3 0.8 collective-permute-start.20
  50.2 1.2 collective-permute-start.17
  51.4 11.4 %attention_backward.2 = (bf16[256,1024]{1,0:T(8,128)(2,1)}, bf16[2,1024,256]{2,1,0:T(8,128)(2,1)}, bf16[256,1024]{1,0:T(8,128)(2,1)}) custom-call(s32[2,8]{1,0:T(2,128)} %bl_ref.5, s32[2]{0:T(128)} %bc_ref.5, s32[3]{0:T(128)} %pad_add_fusion.3.meta_ref, bf16[2,256,1024]{2,1,0:T(8,128)(2,1)} %halve.1.q_ref, bf16[2,256,1024]{2,1,0:T(8,128)(2,1)} %get-tuple-element.83.a_ref, ...), custom_call_target="tpu_custom_call" | custom-call | flops 20000000000 | bytes 1000000 | tf_op jit(solution)/shard_map/attention_backward/pallas_call | solution.py:214
  62.8 1.0 dynamic-slice_bitcast_fusion.4
  63.8 0.9 collective-permute-start.16
  64.7 1.6 %collective-permute-start.21 = (bf16[2,512,256]{2,1,0:T(8,128)(2,1)S(1)}, bf16[2,512,256]{2,1,0:T(8,128)(2,1)S(1)}, u32[]{:S(2)}, u32[]{:S(2)}) collective-permute-start(bf16[2,512,256]{2,1,0:T(8,128)(2,1)S(1)} %copy-done.21), channel_id=1, source_target_pairs={{0,4},{1,5},{2,6},{3,7},{4,0},{5,1},{6,2},{7,3},{8,12},{9,13},{10,... | collective-permute-start | bytes 1572872 | tf_op jit(solution)/shard_map/ppermute | solution.py:365
  67.4 7.2 %attention_backward.3 = (bf16[256,1024]{1,0:T(8,128)(2,1)}, bf16[2,1024,256]{2,1,0:T(8,128)(2,1)}) custom-call(s32[2,8]{1,0:T(2,128)} %bl_ref.5, s32[2]{0:T(128)} %bc_ref.5, s32[3]{0:T(128)} %pad_add_fusion.3.meta_ref, bf16[2,256,1024]{2,1,0:T(8,128)(2,1)} %halve.1.q_ref, bf16[2,256,1024]{2,1,0:T(8,128)(2,1)} %get-tuple-element.83.a_ref, ...), custom_call_target="tpu_custom_call" | custom-call | flops 20000000000 | bytes 1000000 | tf_op jit(solution)/shard_map/attention_backward/pallas_call | solution.py:214
  74.6 1.0 dynamic-slice_bitcast_fusion.3
  76.5 0.7 copy-done.24
  77.6 0.8 copy-done.27
  78.4 5.9 %proj_parts.1 = (bf16[512,256]{1,0:T(8,128)(2,1)}, bf16[512,256]{1,0:T(8,128)(2,1)}, bf16[512,256]{1,0:T(8,128)(2,1)}, bf16[512,256]{1,0:T(8,128)(2,1)}, bf16[51...) custom-call(s32[2,2,2,2]{3,2,1,0:T(2,128)} %pad_add_fusion.cols_ref, ...), custom_call_target="tpu_custom_call" | custom-call | flops 20000000000 | bytes 1000000 | tf_op jit(solution)/shard_map/proj_parts/pallas_call | solution.py:311
  84.4 0.8 collective-permute-start.29
  85.1 1.2 collective-permute-start.30
  86.4 7.0 %mix.1 = (f32[256,2048]{1,0:T(8,128)}, bf16[256,2048]{1,0:T(8,128)(2,1)}) custom-call(s32[3]{0:T(128)} %pad_add_fusion.3.meta_ref, bf16[2,256,1024]{2,1,0:T(8,128)(2,1)} %get-tuple-element.83.a_ref, bf16[256,2048]{1,0:T(8,128)(2,1)} %bitcast.105, bf16[1024,256]{1,0:T(8,128)(2,1)} %copy-done.5, bf16[1024,256]{1,0:T(8,128)(2,1)} %copy-done.16, ...), custom_call_target="tpu_custom_call" | custom-call | flops 20000000000 | bytes 1000000 | tf_op jit(solution)/shard_map/mix/pallas_call | solution.py:283
  93.5 1.0 collective-permute-start.31
  94.5 1.0 collective-permute-start.32
  96.1 1.3 collective-permute-start.26
  97.8 1.2 collective-permute-start.24
  99.0 3.8 %collective-permute-done.32 = bf16[512,256]{1,0:T(8,128)(2,1)S(1)} collective-permute-done((bf16[512,256]{1,0:T(8,128)(2,1)S(1)}, bf16[512,256]{1,0:T(8,128)(2,1)S(1)}, u32[]{:S(2)}, u32[]{:S(2)}) %collective-permute-start.32) | collective-permute-done | bytes 262176 | tf_op jit(solution)/shard_map/ppermute | solution.py:518
  103.3 0.8 collective-permute-start.34
  104.1 7.6 %collective-permute-start.35 = (bf16[512,256]{1,0:T(8,128)(2,1)S(1)}, bf16[512,256]{1,0:T(8,128)(2,1)S(1)}, u32[]{:S(2)}, u32[]{:S(2)}) collective-permute-start(bf16[512,256]{1,0:T(8,128)(2,1)S(1)} %get-tuple-element.113), channel_id=1, source_target_pairs={{0,8},{1,9},{2,10},{3,11},{4,12},{5,13},{6,14},{7,15}} | collective-permute-start | bytes 786440 | tf_op jit(solution)/shard_map/ppermute | solution.py:453
  111.7 3.8 %collective-permute-done.26 = bf16[2,2,256,256]{3,2,1,0:T(8,128)(2,1)S(1)} collective-permute-done((bf16[2,2,256,256]{3,2,1,0:T(8,128)(2,1)S(1)}, bf16[2,2,256,256]{3,2,1,0:T(8,128)(2,1)S(1)}, u32[]{:S(2)}, u32[]{:S(2)}) %collective-permute-start.26) | collective-permute-done | bytes 524320 | tf_op jit(solution)/shard_map/ppermute | solution.py:477
  115.7 1.3 collective-permute-start.27
  117.0 1.4 maximum_select_fusion
  119.3 12.5 %collective-permute-start.37 = (bf16[512,256]{1,0:T(8,128)(2,1)S(1)}, bf16[512,256]{1,0:T(8,128)(2,1)S(1)}, u32[]{:S(2)}, u32[]{:S(2)}) collective-permute-start(bf16[512,256]{1,0:T(8,128)(2,1)S(1)} %get-tuple-element.111), channel_id=1, source_target_pairs={{0,8},{8,16},{1,9},{9,17},{2,10},{10,18},{3,11},{11,19},{4,12},{12... | collective-permute-start | bytes 786440 | tf_op jit(solution)/shard_map/ppermute | solution.py:453
  131.8 0.9 collective-permute-done.27
  132.9 0.8 fusion.13
  133.8 4.2 %collective-permute-done.37 = bf16[512,256]{1,0:T(8,128)(2,1)S(1)} collective-permute-done((bf16[512,256]{1,0:T(8,128)(2,1)S(1)}, bf16[512,256]{1,0:T(8,128)(2,1)S(1)}, u32[]{:S(2)}, u32[]{:S(2)}) %collective-permute-start.37) | collective-permute-done | bytes 262176 | tf_op jit(solution)/shard_map/ppermute | solution.py:453
  138.1 1.3 collective-permute-start.38
  139.4 10.5 %collective-permute-start.39 = (bf16[512,256]{1,0:T(8,128)(2,1)S(1)}, bf16[512,256]{1,0:T(8,128)(2,1)S(1)}, u32[]{:S(2)}, u32[]{:S(2)}) collective-permute-start(bf16[512,256]{1,0:T(8,128)(2,1)S(1)} %get-tuple-element.109), channel_id=1, source_target_pairs={{0,8},{8,16},{16,24},{1,9},{9,17},{17,25},{2,10},{10,18},{18,26},{... | collective-permute-start | bytes 786440 | tf_op jit(solution)/shard_map/ppermute | solution.py:453
  149.9 1.3 fusion
  151.2 1.3 collective-permute-done.38
  152.5 1.2 collective-permute-done.39
  153.8 0.9 convert_add_fusion.6
  (149 shorter events, 16.2 us)
Async XLA Ops:
  0.7 11.7 %copy-start.3 = (bf16[1,256,2048]{2,1,0:T(8,128)(2,1)S(1)}, bf16[1,256,2048]{2,1,0:T(8,128)(2,1)}, u32[]{:S(2)}) copy-start(bf16[1,256,2048]{2,1,0:T(8,128)(2,1)} %param.12) | copy-start | bytes 3145732
  2.1 15.7 %copy-start.5 = (bf16[1024,256]{1,0:T(8,128)(2,1)}, bf16[1024,256]{1,0:T(8,128)(2,1)S(1)}, u32[]{:S(2)}) copy-start(bf16[1024,256]{1,0:T(8,128)(2,1)S(1)} %get-tuple-element.118.rest_6_.rest_0_) | copy-start | bytes 1572868
  2.1 17.0 %collective-permute-start.11 = (bf16[1024,256]{1,0:T(8,128)(2,1)S(1)}, bf16[1024,256]{1,0:T(8,128)(2,1)}, u32[]{:S(2)}, u32[]{:S(2)}) collective-permute-start(bf16[1024,256]{1,0:T(8,128)(2,1)S(1)} %get-tuple-element.118.rest_6_.rest_0_), channel_id=1, source_target_pairs={{0,4},{1,5},{2,6},{3,7},{4,0},{5,1},{6,2},{7,3},{8,12},{9,13},{10,... | collective-permute-start | bytes 1572872 | tf_op jit(solution)/shard_map/ppermute | solution.py:365
  5.1 15.2 %collective-permute-start.10 = (bf16[1024,256]{1,0:T(8,128)(2,1)S(1)}, bf16[1024,256]{1,0:T(8,128)(2,1)}, u32[]{:S(2)}, u32[]{:S(2)}) collective-permute-start(bf16[1024,256]{1,0:T(8,128)(2,1)S(1)} %get-tuple-element.118.rest_6_.rest_0_), channel_id=1, source_target_pairs={{0,2},{1,3},{2,0},{3,1},{4,6},{5,7},{6,4},{7,5},{8,10},{9,11},{10,... | collective-permute-start | bytes 1572872 | tf_op jit(solution)/shard_map/ppermute | solution.py:365
  6.6 5.8 %collective-permute-start.5 = (bf16[1024,256]{1,0:T(8,128)(2,1)S(1)}, bf16[1024,256]{1,0:T(8,128)(2,1)S(1)}, u32[]{:S(2)}, u32[]{:S(2)}) collective-permute-start(bf16[1024,256]{1,0:T(8,128)(2,1)S(1)} %get-tuple-element.119), channel_id=1, source_target_pairs={{0,1},{1,0},{2,3},{3,2},{4,5},{5,4},{6,7},{7,6},{8,9},{9,8},{10,11... | collective-permute-start | bytes 1572872 | tf_op jit(solution)/shard_map/ppermute | solution.py:362
  6.7 5.7 %collective-permute-start.2 = (bf16[256,512]{1,0:T(8,128)(2,1)S(1)}, bf16[256,512]{1,0:T(8,128)(2,1)S(1)}, u32[]{:S(2)}, u32[]{:S(2)}) collective-permute-start(bf16[256,512]{1,0:T(8,128)(2,1)S(1)} %pad_maximum_fusion.9), channel_id=1, source_target_pairs={{0,1},{1,0},{2,3},{3,2},{4,5},{5,4},{6,7},{7,6},{8,9},{9,8},{10,11... | collective-permute-start | bytes 786440 | tf_op jit(solution)/shard_map/ppermute | solution.py:362
  8.0 10.5 %collective-permute-start = (bf16[256,512]{1,0:T(8,128)(2,1)}, bf16[256,512]{1,0:T(8,128)(2,1)}, u32[]{:S(2)}, u32[]{:S(2)}) collective-permute-start(bf16[256,512]{1,0:T(8,128)(2,1)} %pad_maximum_fusion.8.rest_0_), channel_id=1, source_target_pairs={{0,8},{8,16},{16,24},{1,9},{9,17},{17,25},{2,10},{10,18},{18,26},{... | collective-permute-start | bytes 786440 | tf_op jit(solution)/shard_map/ppermute | solution.py:379
  12.4 11.4 %collective-permute-start.6 = (bf16[256,2048]{1,0:T(8,128)(2,1)S(1)}, bf16[256,2048]{1,0:T(8,128)(2,1)}, u32[]{:S(2)}, u32[]{:S(2)}) collective-permute-start(bf16[256,2048]{1,0:T(8,128)(2,1)S(1)} %bitcast.100), channel_id=1, source_target_pairs={{0,1},{1,0},{2,3},{3,2},{4,5},{5,4},{6,7},{7,6},{8,9},{9,8},{10,11... | collective-permute-start | bytes 3145736 | tf_op jit(solution)/shard_map/ppermute | solution.py:362
  13.5 9.6 %collective-permute-start.3 = (bf16[256,512]{1,0:T(8,128)(2,1)}, bf16[256,512]{1,0:T(8,128)(2,1)}, u32[]{:S(2)}, u32[]{:S(2)}) collective-permute-start(bf16[256,512]{1,0:T(8,128)(2,1)} %copy-done.28), channel_id=1, source_target_pairs={{0,8},{8,16},{16,24},{1,9},{9,17},{17,25},{2,10},{10,18},{18,26},{... | collective-permute-start | bytes 786440 | tf_op jit(solution)/shard_map/ppermute | solution.py:379
  18.4 6.4 %collective-permute-start.1 = (bf16[256,512]{1,0:T(8,128)(2,1)}, bf16[256,512]{1,0:T(8,128)(2,1)S(1)}, u32[]{:S(2)}, u32[]{:S(2)}) collective-permute-start(bf16[256,512]{1,0:T(8,128)(2,1)} %collective-permute-done.rest_1_), channel_id=1, source_target_pairs={{8,16},{16,24},{9,17},{17,25},{10,18},{18,26},{11,19},{19,27},{12,... | collective-permute-start | bytes 786440 | tf_op jit(solution)/shard_map/ppermute | solution.py:379
  19.1 13.0 %collective-permute-start.13 = (bf16[1024,256]{1,0:T(8,128)(2,1)}, bf16[1024,256]{1,0:T(8,128)(2,1)S(1)}, u32[]{:S(2)}, u32[]{:S(2)}) collective-permute-start(bf16[1024,256]{1,0:T(8,128)(2,1)} %copy-done.16), channel_id=1, source_target_pairs={{0,4},{1,5},{2,6},{3,7},{4,0},{5,1},{6,2},{7,3},{8,12},{9,13},{10,... | collective-permute-start | bytes 1572872 | tf_op jit(solution)/shard_map/ppermute | solution.py:365
  20.3 12.6 %collective-permute-start.12 = (bf16[1024,256]{1,0:T(8,128)(2,1)}, bf16[1024,256]{1,0:T(8,128)(2,1)S(1)}, u32[]{:S(2)}, u32[]{:S(2)}) collective-permute-start(bf16[1024,256]{1,0:T(8,128)(2,1)} %copy-done.16), channel_id=1, source_target_pairs={{0,2},{1,3},{2,0},{3,1},{4,6},{5,7},{6,4},{7,5},{8,10},{9,11},{10,... | collective-permute-start | bytes 1572872 | tf_op jit(solution)/shard_map/ppermute | solution.py:365
  23.1 3.4 %collective-permute-start.4 = (bf16[256,512]{1,0:T(8,128)(2,1)}, bf16[256,512]{1,0:T(8,128)(2,1)S(1)}, u32[]{:S(2)}, u32[]{:S(2)}) collective-permute-start(bf16[256,512]{1,0:T(8,128)(2,1)} %collective-permute-done.3.rest_5_.rest_1_), channel_id=1, source_target_pairs={{8,16},{16,24},{9,17},{17,25},{10,18},{18,26},{11,19},{19,27},{12,... | collective-permute-start | bytes 786440 | tf_op jit(solution)/shard_map/ppermute | solution.py:379
  23.8 11.3 %collective-permute-start.7 = (bf16[256,2048]{1,0:T(8,128)(2,1)}, bf16[256,2048]{1,0:T(8,128)(2,1)S(1)}, u32[]{:S(2)}, u32[]{:S(2)}) collective-permute-start(bf16[256,2048]{1,0:T(8,128)(2,1)} %bitcast.103), channel_id=1, source_target_pairs={{0,1},{1,0},{2,3},{3,2},{4,5},{5,4},{6,7},{7,6},{8,9},{9,8},{10,11... | collective-permute-start | bytes 3145736 | tf_op jit(solution)/shard_map/ppermute | solution.py:362
  24.9 14.1 %copy-start.29 = (bf16[256,512]{1,0:T(8,128)(2,1)}, bf16[256,512]{1,0:T(8,128)(2,1)S(1)}, u32[]{:S(2)}) copy-start(bf16[256,512]{1,0:T(8,128)(2,1)S(1)} %collective-permute-done.1.rest_2_) | copy-start | bytes 786436
  24.9 14.1 %collective-permute-start.8 = (bf16[256,512]{1,0:T(8,128)(2,1)S(1)}, bf16[256,512]{1,0:T(8,128)(2,1)S(1)}, u32[]{:S(2)}, u32[]{:S(2)}) collective-permute-start(bf16[256,512]{1,0:T(8,128)(2,1)S(1)} %collective-permute-done.1.rest_2_), channel_id=1, source_target_pairs={{16,24},{17,25},{18,26},{19,27},{20,28},{21,29},{22,30},{23,31}} | collective-permute-start | bytes 786440 | tf_op jit(solution)/shard_map/ppermute | solution.py:379
  26.5 12.4 %copy-start.32 = (bf16[256,512]{1,0:T(8,128)(2,1)}, bf16[256,512]{1,0:T(8,128)(2,1)S(1)}, u32[]{:S(2)}) copy-start(bf16[256,512]{1,0:T(8,128)(2,1)S(1)} %collective-permute-done.4.rest_6_.rest_2_) | copy-start | bytes 786436
  26.6 12.5 %collective-permute-start.9 = (bf16[256,512]{1,0:T(8,128)(2,1)S(1)}, bf16[256,512]{1,0:T(8,128)(2,1)S(1)}, u32[]{:S(2)}, u32[]{:S(2)}) collective-permute-start(bf16[256,512]{1,0:T(8,128)(2,1)S(1)} %collective-permute-done.4.rest_6_.rest_2_), channel_id=1, source_target_pairs={{16,24},{17,25},{18,26},{19,27},{20,28},{21,29},{22,30},{23,31}} | collective-permute-start | bytes 786440 | tf_op jit(solution)/shard_map/ppermute | solution.py:379
  32.9 16.4 %collective-permute-start.15 = (bf16[2,512,256]{2,1,0:T(8,128)(2,1)S(1)}, bf16[2,512,256]{2,1,0:T(8,128)(2,1)S(1)}, u32[]{:S(2)}, u32[]{:S(2)}) collective-permute-start(bf16[2,512,256]{2,1,0:T(8,128)(2,1)S(1)} %pad_maximum_fusion.4), channel_id=1, source_target_pairs={{0,2},{1,3},{2,0},{3,1},{4,6},{5,7},{6,4},{7,5},{8,10},{9,11},{10,... | collective-permute-start | bytes 1572872 | tf_op jit(solution)/shard_map/ppermute | solution.py:365
  33.8 15.5 %collective-permute-start.14 = (bf16[2,512,256]{2,1,0:T(8,128)(2,1)S(1)}, bf16[2,512,256]{2,1,0:T(8,128)(2,1)S(1)}, u32[]{:S(2)}, u32[]{:S(2)}) collective-permute-start(bf16[2,512,256]{2,1,0:T(8,128)(2,1)S(1)} %pad_maximum_fusion.3), channel_id=1, source_target_pairs={{0,4},{1,5},{2,6},{3,7},{4,0},{5,1},{6,2},{7,3},{8,12},{9,13},{10,... | collective-permute-start | bytes 1572872 | tf_op jit(solution)/shard_map/ppermute | solution.py:365
  49.3 15.3 %collective-permute-start.20 = (bf16[256,1024]{1,0:T(8,128)(2,1)S(1)}, bf16[256,1024]{1,0:T(8,128)(2,1)S(1)}, u32[]{:S(2)}, u32[]{:S(2)}) collective-permute-start(bf16[256,1024]{1,0:T(8,128)(2,1)S(1)} %get-tuple-element.79), channel_id=1, source_target_pairs={{0,4},{1,5},{2,6},{3,7},{4,0},{5,1},{6,2},{7,3},{8,12},{9,13},{10,... | collective-permute-start | bytes 1572872 | tf_op jit(solution)/shard_map/ppermute | solution.py:365
  50.2 16.1 %collective-permute-start.17 = (bf16[256,1024]{1,0:T(8,128)(2,1)S(1)}, bf16[256,1024]{1,0:T(8,128)(2,1)S(1)}, u32[]{:S(2)}, u32[]{:S(2)}) collective-permute-start(bf16[256,1024]{1,0:T(8,128)(2,1)S(1)} %get-tuple-element.75), channel_id=1, source_target_pairs={{0,2},{1,3},{2,0},{3,1},{4,6},{5,7},{6,4},{7,5},{8,10},{9,11},{10,... | collective-permute-start | bytes 1572872 | tf_op jit(solution)/shard_map/ppermute | solution.py:365
  51.4 13.3 %copy-start.21 = (bf16[2,512,256]{2,1,0:T(8,128)(2,1)S(1)}, bf16[2,512,256]{2,1,0:T(8,128)(2,1)}, u32[]{:S(2)}) copy-start(bf16[2,512,256]{2,1,0:T(8,128)(2,1)} %get-tuple-element.80.refs_4_) | copy-start | bytes 1572868
  51.4 14.9 %copy-start.20 = (bf16[2,512,256]{2,1,0:T(8,128)(2,1)S(1)}, bf16[2,512,256]{2,1,0:T(8,128)(2,1)}, u32[]{:S(2)}) copy-start(bf16[2,512,256]{2,1,0:T(8,128)(2,1)} %get-tuple-element.76.refs_0_) | copy-start | bytes 1572868
  63.8 11.8 %collective-permute-start.16 = (bf16[1,2,256,256]{3,2,1,0:T(8,128)(2,1)S(1)}, bf16[1,2,256,256]{3,2,1,0:T(8,128)(2,1)S(1)}, u32[]{:S(2)}, u32[]{:S(2)}) collective-permute-start(bf16[1,2,256,256]{3,2,1,0:T(8,128)(2,1)S(1)} %dynamic-slice_bitcast_fusion.4), channel_id=1, source_target_pairs={{24,16},{25,17},{26,18},{27,19},{28,20},{29,21},{30,22},{31,23}} | collective-permute-start | bytes 786440 | tf_op jit(solution)/shard_map/ppermute | solution.py:477
  64.7 11.8 %collective-permute-start.21 = (bf16[2,512,256]{2,1,0:T(8,128)(2,1)S(1)}, bf16[2,512,256]{2,1,0:T(8,128)(2,1)S(1)}, u32[]{:S(2)}, u32[]{:S(2)}) collective-permute-start(bf16[2,512,256]{2,1,0:T(8,128)(2,1)S(1)} %copy-done.21), channel_id=1, source_target_pairs={{0,4},{1,5},{2,6},{3,7},{4,0},{5,1},{6,2},{7,3},{8,12},{9,13},{10,... | collective-permute-start | bytes 1572872 | tf_op jit(solution)/shard_map/ppermute | solution.py:365
  66.3 10.2 %collective-permute-start.18 = (bf16[2,512,256]{2,1,0:T(8,128)(2,1)S(1)}, bf16[2,512,256]{2,1,0:T(8,128)(2,1)S(1)}, u32[]{:S(2)}, u32[]{:S(2)}) collective-permute-start(bf16[2,512,256]{2,1,0:T(8,128)(2,1)S(1)} %copy-done.20), channel_id=1, source_target_pairs={{0,2},{1,3},{2,0},{3,1},{4,6},{5,7},{6,4},{7,5},{8,10},{9,11},{10,... | collective-permute-start | bytes 1572872 | tf_op jit(solution)/shard_map/ppermute | solution.py:365
  66.9 9.6 %collective-permute-start.22 = (bf16[256,1024]{1,0:T(8,128)(2,1)S(1)}, bf16[256,1024]{1,0:T(8,128)(2,1)S(1)}, u32[]{:S(2)}, u32[]{:S(2)}) collective-permute-start(bf16[256,1024]{1,0:T(8,128)(2,1)S(1)} %collective-permute-done.20.refs_6_), channel_id=1, source_target_pairs={{0,1},{1,0},{2,3},{3,2},{4,5},{5,4},{6,7},{7,6},{8,9},{9,8},{10,11... | collective-permute-start | bytes 1572872 | tf_op jit(solution)/shard_map/ppermute | solution.py:362
  66.9 9.6 %collective-permute-start.19 = (bf16[256,1024]{1,0:T(8,128)(2,1)S(1)}, bf16[256,1024]{1,0:T(8,128)(2,1)S(1)}, u32[]{:S(2)}, u32[]{:S(2)}) collective-permute-start(bf16[256,1024]{1,0:T(8,128)(2,1)S(1)} %collective-permute-done.17.refs_2_), channel_id=1, source_target_pairs={{0,1},{1,0},{2,3},{3,2},{4,5},{5,4},{6,7},{7,6},{8,9},{9,8},{10,11... | collective-permute-start | bytes 1572872 | tf_op jit(solution)/shard_map/ppermute | solution.py:362
  75.8 18.7 %collective-permute-start.25 = (bf16[2,2,256,256]{3,2,1,0:T(8,128)(2,1)S(1)}, bf16[2,2,256,256]{3,2,1,0:T(8,128)(2,1)S(1)}, u32[]{:S(2)}, u32[]{:S(2)}) collective-permute-start(bf16[2,2,256,256]{3,2,1,0:T(8,128)(2,1)S(1)} %pad_maximum_fusion.5), channel_id=1, source_target_pairs={{16,8},{24,16},{17,9},{25,17},{18,10},{26,18},{19,11},{27,19},{20,... | collective-permute-start | bytes 1572872 | tf_op jit(solution)/shard_map/ppermute | solution.py:477
  84.4 11.3 %collective-permute-start.29 = (bf16[512,256]{1,0:T(8,128)(2,1)}, bf16[512,256]{1,0:T(8,128)(2,1)S(1)}, u32[]{:S(2)}, u32[]{:S(2)}) collective-permute-start(bf16[512,256]{1,0:T(8,128)(2,1)} %get-tuple-element.90), channel_id=1, source_target_pairs={{0,4},{1,5},{2,6},{3,7},{4,0},{5,1},{6,2},{7,3},{8,12},{9,13},{10,... | collective-permute-start | bytes 786440 | tf_op jit(solution)/shard_map/ppermute | solution.py:365
  85.1 11.0 %collective-permute-start.30 = (bf16[512,256]{1,0:T(8,128)(2,1)}, bf16[512,256]{1,0:T(8,128)(2,1)S(1)}, u32[]{:S(2)}, u32[]{:S(2)}) collective-permute-start(bf16[512,256]{1,0:T(8,128)(2,1)} %get-tuple-element.93), channel_id=1, source_target_pairs={{0,2},{1,3},{2,0},{3,1},{4,6},{5,7},{6,4},{7,5},{8,10},{9,11},{10,... | collective-permute-start | bytes 786440 | tf_op jit(solution)/shard_map/ppermute | solution.py:365
  86.4 11.4 %collective-permute-start.33 = (bf16[512,256]{1,0:T(8,128)(2,1)}, bf16[512,256]{1,0:T(8,128)(2,1)S(1)}, u32[]{:S(2)}, u32[]{:S(2)}) collective-permute-start(bf16[512,256]{1,0:T(8,128)(2,1)} %get-tuple-element.100), channel_id=1, source_target_pairs={{0,3},{1,2},{2,1},{3,0},{4,7},{5,6},{6,5},{7,4},{8,11},{9,10},{10,... | collective-permute-start | bytes 786440 | tf_op jit(solution)/shard_map/ppermute | solution.py:518
  93.5 9.5 %collective-permute-start.31 = (bf16[1024,256]{1,0:T(8,128)(2,1)S(1)}, bf16[1024,256]{1,0:T(8,128)(2,1)S(1)}, u32[]{:S(2)}, u32[]{:S(2)}) collective-permute-start(bf16[1024,256]{1,0:T(8,128)(2,1)S(1)} %pad_maximum_fusion.7), channel_id=1, source_target_pairs={{0,1},{1,0},{2,3},{3,2},{4,5},{5,4},{6,7},{7,6},{8,9},{9,8},{10,11... | collective-permute-start | bytes 1572872 | tf_op jit(solution)/shard_map/ppermute | solution.py:362
  94.5 8.3 %collective-permute-start.32 = (bf16[512,256]{1,0:T(8,128)(2,1)S(1)}, bf16[512,256]{1,0:T(8,128)(2,1)S(1)}, u32[]{:S(2)}, u32[]{:S(2)}) collective-permute-start(bf16[512,256]{1,0:T(8,128)(2,1)S(1)} %copy-done.31), channel_id=1, source_target_pairs={{0,5},{1,4},{2,7},{3,6},{4,1},{5,0},{6,3},{7,2},{8,13},{9,12},{10,... | collective-permute-start | bytes 786440 | tf_op jit(solution)/shard_map/ppermute | solution.py:518
  95.6 54.3 %collective-permute-start.23 = (bf16[256,2048]{1,0:T(8,128)(2,1)S(1)}, bf16[256,2048]{1,0:T(8,128)(2,1)S(1)}, u32[]{:S(2)}, u32[]{:S(2)}) collective-permute-start(bf16[256,2048]{1,0:T(8,128)(2,1)S(1)} %copy-done.14), channel_id=1, source_target_pairs={{0,1},{1,0},{2,3},{3,2},{4,5},{5,4},{6,7},{7,6},{8,9},{9,8},{10,11... | collective-permute-start | bytes 3145736 | tf_op jit(solution)/shard_map/ppermute | solution.py:362
  96.1 19.4 %collective-permute-start.26 = (bf16[2,2,256,256]{3,2,1,0:T(8,128)(2,1)S(1)}, bf16[2,2,256,256]{3,2,1,0:T(8,128)(2,1)S(1)}, u32[]{:S(2)}, u32[]{:S(2)}) collective-permute-start(bf16[2,2,256,256]{3,2,1,0:T(8,128)(2,1)S(1)} %pad_maximum_fusion.6), channel_id=1, source_target_pairs={{8,0},{16,8},{24,16},{9,1},{17,9},{25,17},{10,2},{18,10},{26,18},{... | collective-permute-start | bytes 1572872 | tf_op jit(solution)/shard_map/ppermute | solution.py:477
  97.8 19.2 %collective-permute-start.24 = (bf16[256,1024]{1,0:T(8,128)(2,1)S(1)}, bf16[256,1024]{1,0:T(8,128)(2,1)S(1)}, u32[]{:S(2)}, u32[]{:S(2)}) collective-permute-start(bf16[256,1024]{1,0:T(8,128)(2,1)S(1)} %copy-done.17), channel_id=1, source_target_pairs={{0,1},{1,0},{2,3},{3,2},{4,5},{5,4},{6,7},{7,6},{8,9},{9,8},{10,11... | collective-permute-start | bytes 1572872 | tf_op jit(solution)/shard_map/ppermute | solution.py:362
  103.1 13.9 %copy-start.4 = (bf16[256,1024]{1,0:T(8,128)(2,1)S(1)}, bf16[256,1024]{1,0:T(8,128)(2,1)}, u32[]{:S(2)}) copy-start(bf16[256,1024]{1,0:T(8,128)(2,1)} %get-tuple-element.86) | copy-start | bytes 1572868
  103.3 15.2 %collective-permute-start.34 = (bf16[512,256]{1,0:T(8,128)(2,1)S(1)}, bf16[512,256]{1,0:T(8,128)(2,1)S(1)}, u32[]{:S(2)}, u32[]{:S(2)}) collective-permute-start(bf16[512,256]{1,0:T(8,128)(2,1)S(1)} %get-tuple-element.114), channel_id=1, source_target_pairs={{24,16},{25,17},{26,18},{27,19},{28,20},{29,21},{30,22},{31,23}} | collective-permute-start | bytes 786440 | tf_op jit(solution)/shard_map/ppermute | solution.py:453
  104.1 14.4 %collective-permute-start.35 = (bf16[512,256]{1,0:T(8,128)(2,1)S(1)}, bf16[512,256]{1,0:T(8,128)(2,1)S(1)}, u32[]{:S(2)}, u32[]{:S(2)}) collective-permute-start(bf16[512,256]{1,0:T(8,128)(2,1)S(1)} %get-tuple-element.113), channel_id=1, source_target_pairs={{0,8},{1,9},{2,10},{3,11},{4,12},{5,13},{6,14},{7,15}} | collective-permute-start | bytes 786440 | tf_op jit(solution)/shard_map/ppermute | solution.py:453
  115.7 17.1 %collective-permute-start.27 = (bf16[1,2,256,256]{3,2,1,0:T(8,128)(2,1)S(1)}, bf16[1,2,256,256]{3,2,1,0:T(8,128)(2,1)S(1)}, u32[]{:S(2)}, u32[]{:S(2)}) collective-permute-start(bf16[1,2,256,256]{3,2,1,0:T(8,128)(2,1)S(1)} %get-tuple-element.124), channel_id=1, source_target_pairs={{8,0},{16,8},{24,16},{9,1},{17,9},{25,17},{10,2},{18,10},{26,18},{... | collective-permute-start | bytes 786440 | tf_op jit(solution)/shard_map/ppermute | solution.py:477
  117.0 15.8 %collective-permute-start.28 = (bf16[2,256,256]{2,1,0:T(8,128)(2,1)S(1)}, bf16[2,256,256]{2,1,0:T(8,128)(2,1)S(1)}, u32[]{:S(2)}, u32[]{:S(2)}) collective-permute-start(bf16[2,256,256]{2,1,0:T(8,128)(2,1)S(1)} %get-tuple-element.125), channel_id=1, source_target_pairs={{0,1},{1,0},{2,3},{3,2},{4,5},{5,4},{6,7},{7,6},{8,9},{9,8},{10,11... | collective-permute-start | bytes 786440 | tf_op jit(solution)/shard_map/ppermute | solution.py:362
  118.6 15.2 %collective-permute-start.36 = (bf16[512,256]{1,0:T(8,128)(2,1)S(1)}, bf16[512,256]{1,0:T(8,128)(2,1)S(1)}, u32[]{:S(2)}, u32[]{:S(2)}) collective-permute-start(bf16[512,256]{1,0:T(8,128)(2,1)S(1)} %get-tuple-element.112), channel_id=1, source_target_pairs={{16,8},{24,16},{17,9},{25,17},{18,10},{26,18},{19,11},{27,19},{20,... | collective-permute-start | bytes 786440 | tf_op jit(solution)/shard_map/ppermute | solution.py:453
  119.3 30.6 %copy-start = (f32[256,2048]{1,0:T(8,128)S(1)}, f32[256,2048]{1,0:T(8,128)}, u32[]{:S(2)}) copy-start(f32[256,2048]{1,0:T(8,128)} %get-tuple-element.84) | copy-start | bytes 6291460
  119.3 18.7 %collective-permute-start.37 = (bf16[512,256]{1,0:T(8,128)(2,1)S(1)}, bf16[512,256]{1,0:T(8,128)(2,1)S(1)}, u32[]{:S(2)}, u32[]{:S(2)}) collective-permute-start(bf16[512,256]{1,0:T(8,128)(2,1)S(1)} %get-tuple-element.111), channel_id=1, source_target_pairs={{0,8},{8,16},{1,9},{9,17},{2,10},{10,18},{3,11},{11,19},{4,12},{12... | collective-permute-start | bytes 786440 | tf_op jit(solution)/shard_map/ppermute | solution.py:453
  138.1 14.4 %collective-permute-start.38 = (bf16[512,256]{1,0:T(8,128)(2,1)S(1)}, bf16[512,256]{1,0:T(8,128)(2,1)S(1)}, u32[]{:S(2)}, u32[]{:S(2)}) collective-permute-start(bf16[512,256]{1,0:T(8,128)(2,1)S(1)} %get-tuple-element.110), channel_id=1, source_target_pairs={{8,0},{16,8},{24,16},{9,1},{17,9},{25,17},{10,2},{18,10},{26,18},{... | collective-permute-start | bytes 786440 | tf_op jit(solution)/shard_map/ppermute | solution.py:453
  139.4 14.4 %collective-permute-start.39 = (bf16[512,256]{1,0:T(8,128)(2,1)S(1)}, bf16[512,256]{1,0:T(8,128)(2,1)S(1)}, u32[]{:S(2)}, u32[]{:S(2)}) collective-permute-start(bf16[512,256]{1,0:T(8,128)(2,1)S(1)} %get-tuple-element.109), channel_id=1, source_target_pairs={{0,8},{8,16},{16,24},{1,9},{9,17},{17,25},{2,10},{10,18},{18,26},{... | collective-permute-start | bytes 786440 | tf_op jit(solution)/shard_map/ppermute | solution.py:453
  (26 other events, 119.9 us)
where the time goes:
time: 157 us; the launch traced here: 155 us
  starting transfers between devices  66.9 us (43%)
  Pallas kernels  43.3 us (28%)
  waiting for transfers between devices  24.2 us (15%)
  local copies, waits for them, and re-layouts  11.4 us (7%)
  other arithmetic  7.45 us (5%)
    ppermute x6, starting transfers between devices, send(): self.got = lax.ppermute(self.sent, 'ctx', pairs)  33.3 us
    pallas_call x2, Pallas kernels, backward(): pl.pallas_call(functools.partial(backward_kernel, nc, nb, plan, width), g...  18.6 us
    ppermute x12, starting transfers between devices, to_chip(): return lax.ppermute(x, 'fsdp', [(p, p ^ 2 * bit) for p in range(nf)])  14.1 us
    ppermute x6, starting transfers between devices, hop_up(): return lax.ppermute(x, 'ctx', [(p, p + 1) for p in range(step - 1, nc - 1)])  10.4 us
    pallas_call x1, Pallas kernels, forward(): pl.pallas_call(functools.partial(forward_kernel, nc, nb), grid_spec=pltpu...  8.85 us
    pallas_call x1, Pallas kernels, mix(): pl.pallas_call(functools.partial(mix_kernel, plan, width), in_specs=[pl.B...  7.01 us
    ppermute x6, waiting for transfers between devices, send(): self.got = lax.ppermute(self.sent, 'ctx', pairs)  6.77 us
    pallas_call x1, Pallas kernels, proj_parts(): pl.pallas_call(functools.partial(proj_kernel, count, width), in_specs=[pl...  5.94 us
  transfers between devices with their start and end apart: 40, of which 11 were waited for; matrix products, arithmetic and copies ran while one was open for 7% of the time, Pallas kernels for 28%

commit v1 on v0

--- a/solution.py
+++ b/solution.py
@@ -27,6 +27,7 @@
 BF16 = jnp.bfloat16
 VMEM_LIMIT = 56 * 1024 * 1024
 NT = (((1,), (1,)), ((), ()))
+TN = (((0,), (0,)), ((), ()))
 
 
 def dot(a, b):
@@ -69,15 +70,12 @@
 
 
 def by_count(count, run):
-    small = KEY_SLOTS // 2
-
-    @pl.when(count <= small)
-    def _():
-        run(small)
-
-    @pl.when(count > small)
-    def _():
-        run(KEY_SLOTS)
+    quarter = KEY_SLOTS // 4
+    for n in range(1, 5):
+
+        @pl.when((count > (n - 1) * quarter) & (count <= n * quarter))
+        def _(n=n):
+            run(n * quarter)
 
 
 def wide_part(ref, g):
@@ -110,13 +108,13 @@
             top = jnp.max(s_t, axis=0, keepdims=True)
             p = jnp.exp2((s_t - top) * EXP2_SCALE)
             total = jnp.sum(p, axis=0, keepdims=True)
-            a_t = dot(v_cat.T, p.astype(BF16)) / total
+            a_t = lax.dot_general(v_cat, p.astype(BF16), TN, preferred_element_type=F32) / total
             st_ref[0, g] = top * EXP2_SCALE + jnp.log2(total)
             for h in range(GROUP):
                 part = a_t[:, h * BLOCK_SIZE:(h + 1) * BLOCK_SIZE]
                 at_refs[g][0, h * HEAD_DIM:(h + 1) * HEAD_DIM, :] = part.astype(BF16)
                 lane = g * WIDE + h * HEAD_DIM
-                a_ref[0, :, lane:lane + HEAD_DIM] = part.T.astype(BF16)
+                a_ref[0, :, lane:lane + HEAD_DIM] = part.astype(BF16).T
 
     by_count(count, run)
 
@@ -187,11 +185,11 @@
             ds = (p * (dp - row_dot)).astype(BF16)
             dv = dot(p.astype(BF16), dos)
             dk = dot(ds, qs) * SCALE
-            dq_t = dot(k_cat.T, ds) * SCALE
+            dq_t = lax.dot_general(k_cat, ds, TN, preferred_element_type=F32) * SCALE
             for h in range(GROUP):
                 part = dq_t[:, h * BLOCK_SIZE:(h + 1) * BLOCK_SIZE]
                 lane = g * WIDE + h * HEAD_DIM
-                dq_ref[:, lane:lane + HEAD_DIM] = part.T.astype(BF16)
+                dq_ref[:, lane:lane + HEAD_DIM] = part.astype(BF16).T
             lanes = slice(g * HEAD_DIM, (g + 1) * HEAD_DIM)
             for j in range(slots):
                 at = pl.ds(pl.multiple_of(bl_ref[i, j] * BLOCK_SIZE, BLOCK_SIZE), BLOCK_SIZE)

time: 157 us -> 154 us (0.981); the launches traced: 155 us -> 156 us
  starting transfers between devices: 66.9 us -> 70.5 us
  Pallas kernels: 43.3 us -> 39.8 us
    ppermute x6, starting transfers between devices: 33.3 us -> 37.1 us  [send(): self.got = lax.ppermute(self.sent, 'ctx', pairs)]
    pallas_call x2, Pallas kernels: 18.6 us -> 16.5 us  [backward(): pl.pallas_call(functools.partial(backward_kernel, nc, nb, plan, width), g...]
  transfers between devices with their start and end apart: 40 -> 40, of which waited for: 11 -> 11; matrix products, arithmetic and copies ran while one was open for 7% -> 7% of each run, Pallas kernels for 28% -> 26%
where the time goes in v1:
time: 154 us; the launch traced here: 156 us
  starting transfers between devices  70.5 us (46%)
  Pallas kernels  39.8 us (26%)
  waiting for transfers between devices  25.1 us (16%)
  local copies, waits for them, and re-layouts  11.3 us (7%)
  other arithmetic  7.45 us (5%)
    ppermute x6, starting transfers between devices, send(): self.got = lax.ppermute(self.sent, 'ctx', pairs)  37.1 us
    pallas_call x2, Pallas kernels, backward(): pl.pallas_call(functools.partial(backward_kernel, nc, nb, plan, width), g...  16.5 us
    ppermute x12, starting transfers between devices, to_chip(): return lax.ppermute(x, 'fsdp', [(p, p ^ 2 * bit) for p in range(nf)])  13.6 us
    ppermute x6, starting transfers between devices, hop_up(): return lax.ppermute(x, 'ctx', [(p, p + 1) for p in range(step - 1, nc - 1)])  10.4 us
    pallas_call x1, Pallas kernels, forward(): pl.pallas_call(functools.partial(forward_kernel, nc, nb), grid_spec=pltpu...  7.5 us
    pallas_call x1, Pallas kernels, mix(): pl.pallas_call(functools.partial(mix_kernel, plan, width), in_specs=[pl.B...  7.01 us
    ppermute x6, waiting for transfers between devices, send(): self.got = lax.ppermute(self.sent, 'ctx', pairs)  6.77 us
    ppermute x12, waiting for transfers between devices, to_chip(): return lax.ppermute(x, 'fsdp', [(p, p ^ 2 * bit) for p in range(nf)])  6.38 us
  transfers between devices with their start and end apart: 40, of which 11 were waited for; matrix products, arithmetic and copies ran while one was open for 7% of the time, Pallas kernels for 26%

profile of v1, /device:TPU:0, one launch (start us, length us, event | category | flops | bytes accessed | tf_op | source)
XLA Modules:
  0.0 155.5 jit_solution(13518242863679652273)
XLA Ops:
  0.7 1.4 constant_dynamic-slice_fusion.2
  2.1 3.0 %collective-permute-start.11 = (bf16[1024,256]{1,0:T(8,128)(2,1)S(1)}, bf16[1024,256]{1,0:T(8,128)(2,1)}, u32[]{:S(2)}, u32[]{:S(2)}) collective-permute-start(bf16[1024,256]{1,0:T(8,128)(2,1)S(1)} %get-tuple-element.118.rest_6_.rest_0_), channel_id=1, source_target_pairs={{0,4},{1,5},{2,6},{3,7},{4,0},{5,1},{6,2},{7,3},{8,12},{9,13},{10,... | collective-permute-start | bytes 1572872 | tf_op jit(solution)/shard_map/ppermute | solution.py:363
  5.1 1.5 collective-permute-start.10
  8.0 4.2 %collective-permute-start = (bf16[256,512]{1,0:T(8,128)(2,1)}, bf16[256,512]{1,0:T(8,128)(2,1)}, u32[]{:S(2)}, u32[]{:S(2)}) collective-permute-start(bf16[256,512]{1,0:T(8,128)(2,1)} %pad_maximum_fusion.8.rest_0_), channel_id=1, source_target_pairs={{0,8},{8,16},{16,24},{1,9},{9,17},{17,25},{2,10},{10,18},{18,26},{... | collective-permute-start | bytes 786440 | tf_op jit(solution)/shard_map/ppermute | solution.py:377
  13.5 3.5 %collective-permute-start.3 = (bf16[256,512]{1,0:T(8,128)(2,1)}, bf16[256,512]{1,0:T(8,128)(2,1)}, u32[]{:S(2)}, u32[]{:S(2)}) collective-permute-start(bf16[256,512]{1,0:T(8,128)(2,1)} %copy-done.28), channel_id=1, source_target_pairs={{0,8},{8,16},{16,24},{1,9},{9,17},{17,25},{2,10},{10,18},{18,26},{... | collective-permute-start | bytes 786440 | tf_op jit(solution)/shard_map/ppermute | solution.py:377
  21.0 2.1 %collective-permute-done.3.rest_5_.rest_1_ = bf16[256,512]{1,0:T(8,128)(2,1)} collective-permute-done((bf16[256,512]{1,0:T(8,128)(2,1)}, bf16[256,512]{1,0:T(8,128)(2,1)}, u32[]{:S(2)}, u32[]{:S(2)}) %collective-permute-start.3) | collective-permute-done | bytes 262176 | tf_op jit(solution)/shard_map/ppermute | solution.py:377
  23.9 1.0 slice_bitcast_fusion.3
  25.6 1.0 slice_bitcast_fusion.5
  27.2 4.8 %collective-permute-done.13.rest_11_.rest_5_ = bf16[1024,256]{1,0:T(8,128)(2,1)S(1)} collective-permute-done((bf16[1024,256]{1,0:T(8,128)(2,1)}, bf16[1024,256]{1,0:T(8,128)(2,1)S(1)}, u32[]{:S(2)}, u32[]{:S(2)}) %collective-permute-start.13) | collective-permute-done | bytes 524320 | tf_op jit(solution)/shard_map/ppermute | solution.py:363
  32.9 0.8 collective-permute-start.15
  33.8 1.3 collective-permute-start.14
  35.1 1.0 copy-done.15
  36.1 2.9 %halve.1.q_ref = bf16[2,256,1024]{2,1,0:T(8,128)(2,1)} custom-call(s32[3]{0:T(128)} %pad_add_fusion.3.meta_ref, bf16[256,2048]{1,0:T(8,128)(2,1)} %bitcast.104, bf16[256,2048]{1,0:T(8,128)(2,1)} %copy-done.15), custom_call_target="tpu_custom_call" | custom-call | flops 20000000000 | bytes 1000000 | tf_op jit(solution)/shard_map/halve/pallas_call | solution.py:328
  40.4 7.5 %attention_forward.1 = (bf16[2,256,1024]{2,1,0:T(8,128)(2,1)}, bf16[2,512,256]{2,1,0:T(8,128)(2,1)}, bf16[2,512,256]{2,1,0:T(8,128)(2,1)}, f32[4,2,1,512]{3,2,1,0:T(1,128)}) custom-call(s32[2,8]{1,0:T(2,128)} %bl_ref.5, s32[2]{0:T(128)} %bc_ref.5, s32[3]{0:T(128)} %pad_add_fusion.3.meta_ref, bf16[2,256,1024]{2,1,0:T(8,128)(2,1)} %halve.1.q_ref, ...), custom_call_target="tpu_custom_call" | custom-call | flops 20000000000 | bytes 1000000 | tf_op jit(solution)/shard_map/attention_forward/pallas_call | solution.py:131
  48.0 0.8 collective-permute-start.20
  48.8 1.2 collective-permute-start.17
  50.1 10.3 %attention_backward.2 = (bf16[256,1024]{1,0:T(8,128)(2,1)}, bf16[2,1024,256]{2,1,0:T(8,128)(2,1)}, bf16[256,1024]{1,0:T(8,128)(2,1)}) custom-call(s32[2,8]{1,0:T(2,128)} %bl_ref.5, s32[2]{0:T(128)} %bc_ref.5, s32[3]{0:T(128)} %pad_add_fusion.3.meta_ref, bf16[2,256,1024]{2,1,0:T(8,128)(2,1)} %halve.1.q_ref, bf16[2,256,1024]{2,1,0:T(8,128)(2,1)} %get-tuple-element.83.a_ref, ...), custom_call_target="tpu_custom_call" | custom-call | flops 20000000000 | bytes 1000000 | tf_op jit(solution)/shard_map/attention_backward/pallas_call | solution.py:212
  60.4 1.0 dynamic-slice_bitcast_fusion.4
  62.1 1.6 %collective-permute-start.21 = (bf16[2,512,256]{2,1,0:T(8,128)(2,1)S(1)}, bf16[2,512,256]{2,1,0:T(8,128)(2,1)S(1)}, u32[]{:S(2)}, u32[]{:S(2)}) collective-permute-start(bf16[2,512,256]{2,1,0:T(8,128)(2,1)S(1)} %copy-done.21), channel_id=1, source_target_pairs={{0,4},{1,5},{2,6},{3,7},{4,0},{5,1},{6,2},{7,3},{8,12},{9,13},{10,... | collective-permute-start | bytes 1572872 | tf_op jit(solution)/shard_map/ppermute | solution.py:363
  64.8 6.1 %attention_backward.3 = (bf16[256,1024]{1,0:T(8,128)(2,1)}, bf16[2,1024,256]{2,1,0:T(8,128)(2,1)}) custom-call(s32[2,8]{1,0:T(2,128)} %bl_ref.5, s32[2]{0:T(128)} %bc_ref.5, s32[3]{0:T(128)} %pad_add_fusion.3.meta_ref, bf16[2,256,1024]{2,1,0:T(8,128)(2,1)} %halve.1.q_ref, bf16[2,256,1024]{2,1,0:T(8,128)(2,1)} %get-tuple-element.83.a_ref, ...), custom_call_target="tpu_custom_call" | custom-call | flops 20000000000 | bytes 1000000 | tf_op jit(solution)/shard_map/attention_backward/pallas_call | solution.py:212
  71.0 1.0 dynamic-slice_bitcast_fusion.3
  72.1 1.0 collective-permute-start.25
  73.1 0.8 collective-permute-done.18.refs_1_
  73.9 0.8 copy-done.25
  74.8 0.8 copy-done.27
  75.6 5.9 %proj_parts.1 = (bf16[512,256]{1,0:T(8,128)(2,1)}, bf16[512,256]{1,0:T(8,128)(2,1)}, bf16[512,256]{1,0:T(8,128)(2,1)}, bf16[512,256]{1,0:T(8,128)(2,1)}, bf16[51...) custom-call(s32[2,2,2,2]{3,2,1,0:T(2,128)} %pad_add_fusion.cols_ref, ...), custom_call_target="tpu_custom_call" | custom-call | flops 20000000000 | bytes 1000000 | tf_op jit(solution)/shard_map/proj_parts/pallas_call | solution.py:309
  82.1 1.0 collective-permute-start.30
  83.1 7.0 %mix.1 = (f32[256,2048]{1,0:T(8,128)}, bf16[256,2048]{1,0:T(8,128)(2,1)}) custom-call(s32[3]{0:T(128)} %pad_add_fusion.3.meta_ref, bf16[2,256,1024]{2,1,0:T(8,128)(2,1)} %get-tuple-element.83.a_ref, bf16[256,2048]{1,0:T(8,128)(2,1)} %bitcast.105, bf16[1024,256]{1,0:T(8,128)(2,1)} %copy-done.5, bf16[1024,256]{1,0:T(8,128)(2,1)} %copy-done.16, ...), custom_call_target="tpu_custom_call" | custom-call | flops 20000000000 | bytes 1000000 | tf_op jit(solution)/shard_map/mix/pallas_call | solution.py:281
  90.2 1.2 collective-permute-start.31
  91.4 1.2 collective-permute-start.32
  93.4 1.3 collective-permute-start.26
  94.7 1.0 collective-permute-start.24
  95.6 4.1 %collective-permute-done.32 = bf16[512,256]{1,0:T(8,128)(2,1)S(1)} collective-permute-done((bf16[512,256]{1,0:T(8,128)(2,1)S(1)}, bf16[512,256]{1,0:T(8,128)(2,1)S(1)}, u32[]{:S(2)}, u32[]{:S(2)}) %collective-permute-start.32) | collective-permute-done | bytes 262176 | tf_op jit(solution)/shard_map/ppermute | solution.py:516
  100.2 0.8 collective-permute-start.34
  101.0 9.7 %collective-permute-start.35 = (bf16[512,256]{1,0:T(8,128)(2,1)S(1)}, bf16[512,256]{1,0:T(8,128)(2,1)S(1)}, u32[]{:S(2)}, u32[]{:S(2)}) collective-permute-start(bf16[512,256]{1,0:T(8,128)(2,1)S(1)} %get-tuple-element.113), channel_id=1, source_target_pairs={{0,8},{1,9},{2,10},{3,11},{4,12},{5,13},{6,14},{7,15}} | collective-permute-start | bytes 786440 | tf_op jit(solution)/shard_map/ppermute | solution.py:451
  110.7 4.0 %collective-permute-done.26 = bf16[2,2,256,256]{3,2,1,0:T(8,128)(2,1)S(1)} collective-permute-done((bf16[2,2,256,256]{3,2,1,0:T(8,128)(2,1)S(1)}, bf16[2,2,256,256]{3,2,1,0:T(8,128)(2,1)S(1)}, u32[]{:S(2)}, u32[]{:S(2)}) %collective-permute-start.26) | collective-permute-done | bytes 524320 | tf_op jit(solution)/shard_map/ppermute | solution.py:475
  114.9 1.3 collective-permute-start.27
  116.3 1.4 maximum_select_fusion
  118.5 13.8 %collective-permute-start.37 = (bf16[512,256]{1,0:T(8,128)(2,1)S(1)}, bf16[512,256]{1,0:T(8,128)(2,1)S(1)}, u32[]{:S(2)}, u32[]{:S(2)}) collective-permute-start(bf16[512,256]{1,0:T(8,128)(2,1)S(1)} %get-tuple-element.111), channel_id=1, source_target_pairs={{0,8},{8,16},{1,9},{9,17},{2,10},{10,18},{3,11},{11,19},{4,12},{12... | collective-permute-start | bytes 786440 | tf_op jit(solution)/shard_map/ppermute | solution.py:451
  132.4 0.9 collective-permute-done.27
  133.6 0.8 fusion.13
  134.4 4.2 %collective-permute-done.37 = bf16[512,256]{1,0:T(8,128)(2,1)S(1)} collective-permute-done((bf16[512,256]{1,0:T(8,128)(2,1)S(1)}, bf16[512,256]{1,0:T(8,128)(2,1)S(1)}, u32[]{:S(2)}, u32[]{:S(2)}) %collective-permute-start.37) | collective-permute-done | bytes 262176 | tf_op jit(solution)/shard_map/ppermute | solution.py:451
  138.7 1.3 collective-permute-start.38
  140.0 10.8 %collective-permute-start.39 = (bf16[512,256]{1,0:T(8,128)(2,1)S(1)}, bf16[512,256]{1,0:T(8,128)(2,1)S(1)}, u32[]{:S(2)}, u32[]{:S(2)}) collective-permute-start(bf16[512,256]{1,0:T(8,128)(2,1)S(1)} %get-tuple-element.109), channel_id=1, source_target_pairs={{0,8},{8,16},{16,24},{1,9},{9,17},{17,25},{2,10},{10,18},{18,26},{... | collective-permute-start | bytes 786440 | tf_op jit(solution)/shard_map/ppermute | solution.py:451
  150.8 1.3 fusion
  152.1 1.3 collective-permute-done.38
  153.4 1.2 collective-permute-done.39
  154.7 0.9 convert_add_fusion.6
  (149 shorter events, 16.2 us)
Async XLA Ops:
  0.7 11.7 %copy-start.3 = (bf16[1,256,2048]{2,1,0:T(8,128)(2,1)S(1)}, bf16[1,256,2048]{2,1,0:T(8,128)(2,1)}, u32[]{:S(2)}) copy-start(bf16[1,256,2048]{2,1,0:T(8,128)(2,1)} %param.12) | copy-start | bytes 3145732
  2.1 15.7 %copy-start.5 = (bf16[1024,256]{1,0:T(8,128)(2,1)}, bf16[1024,256]{1,0:T(8,128)(2,1)S(1)}, u32[]{:S(2)}) copy-start(bf16[1024,256]{1,0:T(8,128)(2,1)S(1)} %get-tuple-element.118.rest_6_.rest_0_) | copy-start | bytes 1572868
  2.1 17.0 %collective-permute-start.11 = (bf16[1024,256]{1,0:T(8,128)(2,1)S(1)}, bf16[1024,256]{1,0:T(8,128)(2,1)}, u32[]{:S(2)}, u32[]{:S(2)}) collective-permute-start(bf16[1024,256]{1,0:T(8,128)(2,1)S(1)} %get-tuple-element.118.rest_6_.rest_0_), channel_id=1, source_target_pairs={{0,4},{1,5},{2,6},{3,7},{4,0},{5,1},{6,2},{7,3},{8,12},{9,13},{10,... | collective-permute-start | bytes 1572872 | tf_op jit(solution)/shard_map/ppermute | solution.py:363
  5.1 15.2 %collective-permute-start.10 = (bf16[1024,256]{1,0:T(8,128)(2,1)S(1)}, bf16[1024,256]{1,0:T(8,128)(2,1)}, u32[]{:S(2)}, u32[]{:S(2)}) collective-permute-start(bf16[1024,256]{1,0:T(8,128)(2,1)S(1)} %get-tuple-element.118.rest_6_.rest_0_), channel_id=1, source_target_pairs={{0,2},{1,3},{2,0},{3,1},{4,6},{5,7},{6,4},{7,5},{8,10},{9,11},{10,... | collective-permute-start | bytes 1572872 | tf_op jit(solution)/shard_map/ppermute | solution.py:363
  6.6 5.8 %collective-permute-start.5 = (bf16[1024,256]{1,0:T(8,128)(2,1)S(1)}, bf16[1024,256]{1,0:T(8,128)(2,1)S(1)}, u32[]{:S(2)}, u32[]{:S(2)}) collective-permute-start(bf16[1024,256]{1,0:T(8,128)(2,1)S(1)} %get-tuple-element.119), channel_id=1, source_target_pairs={{0,1},{1,0},{2,3},{3,2},{4,5},{5,4},{6,7},{7,6},{8,9},{9,8},{10,11... | collective-permute-start | bytes 1572872 | tf_op jit(solution)/shard_map/ppermute | solution.py:360
  6.7 5.7 %collective-permute-start.2 = (bf16[256,512]{1,0:T(8,128)(2,1)S(1)}, bf16[256,512]{1,0:T(8,128)(2,1)S(1)}, u32[]{:S(2)}, u32[]{:S(2)}) collective-permute-start(bf16[256,512]{1,0:T(8,128)(2,1)S(1)} %pad_maximum_fusion.9), channel_id=1, source_target_pairs={{0,1},{1,0},{2,3},{3,2},{4,5},{5,4},{6,7},{7,6},{8,9},{9,8},{10,11... | collective-permute-start | bytes 786440 | tf_op jit(solution)/shard_map/ppermute | solution.py:360
  8.0 10.5 %collective-permute-start = (bf16[256,512]{1,0:T(8,128)(2,1)}, bf16[256,512]{1,0:T(8,128)(2,1)}, u32[]{:S(2)}, u32[]{:S(2)}) collective-permute-start(bf16[256,512]{1,0:T(8,128)(2,1)} %pad_maximum_fusion.8.rest_0_), channel_id=1, source_target_pairs={{0,8},{8,16},{16,24},{1,9},{9,17},{17,25},{2,10},{10,18},{18,26},{... | collective-permute-start | bytes 786440 | tf_op jit(solution)/shard_map/ppermute | solution.py:377
  12.4 11.4 %collective-permute-start.6 = (bf16[256,2048]{1,0:T(8,128)(2,1)S(1)}, bf16[256,2048]{1,0:T(8,128)(2,1)}, u32[]{:S(2)}, u32[]{:S(2)}) collective-permute-start(bf16[256,2048]{1,0:T(8,128)(2,1)S(1)} %bitcast.100), channel_id=1, source_target_pairs={{0,1},{1,0},{2,3},{3,2},{4,5},{5,4},{6,7},{7,6},{8,9},{9,8},{10,11... | collective-permute-start | bytes 3145736 | tf_op jit(solution)/shard_map/ppermute | solution.py:360
  13.5 9.6 %collective-permute-start.3 = (bf16[256,512]{1,0:T(8,128)(2,1)}, bf16[256,512]{1,0:T(8,128)(2,1)}, u32[]{:S(2)}, u32[]{:S(2)}) collective-permute-start(bf16[256,512]{1,0:T(8,128)(2,1)} %copy-done.28), channel_id=1, source_target_pairs={{0,8},{8,16},{16,24},{1,9},{9,17},{17,25},{2,10},{10,18},{18,26},{... | collective-permute-start | bytes 786440 | tf_op jit(solution)/shard_map/ppermute | solution.py:377
  18.4 6.4 %collective-permute-start.1 = (bf16[256,512]{1,0:T(8,128)(2,1)}, bf16[256,512]{1,0:T(8,128)(2,1)S(1)}, u32[]{:S(2)}, u32[]{:S(2)}) collective-permute-start(bf16[256,512]{1,0:T(8,128)(2,1)} %collective-permute-done.rest_1_), channel_id=1, source_target_pairs={{8,16},{16,24},{9,17},{17,25},{10,18},{18,26},{11,19},{19,27},{12,... | collective-permute-start | bytes 786440 | tf_op jit(solution)/shard_map/ppermute | solution.py:377
  19.1 13.0 %collective-permute-start.13 = (bf16[1024,256]{1,0:T(8,128)(2,1)}, bf16[1024,256]{1,0:T(8,128)(2,1)S(1)}, u32[]{:S(2)}, u32[]{:S(2)}) collective-permute-start(bf16[1024,256]{1,0:T(8,128)(2,1)} %copy-done.16), channel_id=1, source_target_pairs={{0,4},{1,5},{2,6},{3,7},{4,0},{5,1},{6,2},{7,3},{8,12},{9,13},{10,... | collective-permute-start | bytes 1572872 | tf_op jit(solution)/shard_map/ppermute | solution.py:363
  20.3 12.6 %collective-permute-start.12 = (bf16[1024,256]{1,0:T(8,128)(2,1)}, bf16[1024,256]{1,0:T(8,128)(2,1)S(1)}, u32[]{:S(2)}, u32[]{:S(2)}) collective-permute-start(bf16[1024,256]{1,0:T(8,128)(2,1)} %copy-done.16), channel_id=1, source_target_pairs={{0,2},{1,3},{2,0},{3,1},{4,6},{5,7},{6,4},{7,5},{8,10},{9,11},{10,... | collective-permute-start | bytes 1572872 | tf_op jit(solution)/shard_map/ppermute | solution.py:363
  23.1 3.4 %collective-permute-start.4 = (bf16[256,512]{1,0:T(8,128)(2,1)}, bf16[256,512]{1,0:T(8,128)(2,1)S(1)}, u32[]{:S(2)}, u32[]{:S(2)}) collective-permute-start(bf16[256,512]{1,0:T(8,128)(2,1)} %collective-permute-done.3.rest_5_.rest_1_), channel_id=1, source_target_pairs={{8,16},{16,24},{9,17},{17,25},{10,18},{18,26},{11,19},{19,27},{12,... | collective-permute-start | bytes 786440 | tf_op jit(solution)/shard_map/ppermute | solution.py:377
  23.8 11.3 %collective-permute-start.7 = (bf16[256,2048]{1,0:T(8,128)(2,1)}, bf16[256,2048]{1,0:T(8,128)(2,1)S(1)}, u32[]{:S(2)}, u32[]{:S(2)}) collective-permute-start(bf16[256,2048]{1,0:T(8,128)(2,1)} %bitcast.103), channel_id=1, source_target_pairs={{0,1},{1,0},{2,3},{3,2},{4,5},{5,4},{6,7},{7,6},{8,9},{9,8},{10,11... | collective-permute-start | bytes 3145736 | tf_op jit(solution)/shard_map/ppermute | solution.py:360
  24.9 14.1 %copy-start.29 = (bf16[256,512]{1,0:T(8,128)(2,1)}, bf16[256,512]{1,0:T(8,128)(2,1)S(1)}, u32[]{:S(2)}) copy-start(bf16[256,512]{1,0:T(8,128)(2,1)S(1)} %collective-permute-done.1.rest_2_) | copy-start | bytes 786436
  24.9 14.1 %collective-permute-start.8 = (bf16[256,512]{1,0:T(8,128)(2,1)S(1)}, bf16[256,512]{1,0:T(8,128)(2,1)S(1)}, u32[]{:S(2)}, u32[]{:S(2)}) collective-permute-start(bf16[256,512]{1,0:T(8,128)(2,1)S(1)} %collective-permute-done.1.rest_2_), channel_id=1, source_target_pairs={{16,24},{17,25},{18,26},{19,27},{20,28},{21,29},{22,30},{23,31}} | collective-permute-start | bytes 786440 | tf_op jit(solution)/shard_map/ppermute | solution.py:377
  26.5 12.4 %copy-start.32 = (bf16[256,512]{1,0:T(8,128)(2,1)}, bf16[256,512]{1,0:T(8,128)(2,1)S(1)}, u32[]{:S(2)}) copy-start(bf16[256,512]{1,0:T(8,128)(2,1)S(1)} %collective-permute-done.4.rest_6_.rest_2_) | copy-start | bytes 786436
  26.6 12.5 %collective-permute-start.9 = (bf16[256,512]{1,0:T(8,128)(2,1)S(1)}, bf16[256,512]{1,0:T(8,128)(2,1)S(1)}, u32[]{:S(2)}, u32[]{:S(2)}) collective-permute-start(bf16[256,512]{1,0:T(8,128)(2,1)S(1)} %collective-permute-done.4.rest_6_.rest_2_), channel_id=1, source_target_pairs={{16,24},{17,25},{18,26},{19,27},{20,28},{21,29},{22,30},{23,31}} | collective-permute-start | bytes 786440 | tf_op jit(solution)/shard_map/ppermute | solution.py:377
  32.9 15.0 %collective-permute-start.15 = (bf16[2,512,256]{2,1,0:T(8,128)(2,1)S(1)}, bf16[2,512,256]{2,1,0:T(8,128)(2,1)S(1)}, u32[]{:S(2)}, u32[]{:S(2)}) collective-permute-start(bf16[2,512,256]{2,1,0:T(8,128)(2,1)S(1)} %pad_maximum_fusion.4), channel_id=1, source_target_pairs={{0,2},{1,3},{2,0},{3,1},{4,6},{5,7},{6,4},{7,5},{8,10},{9,11},{10,... | collective-permute-start | bytes 1572872 | tf_op jit(solution)/shard_map/ppermute | solution.py:363
  33.8 14.2 %collective-permute-start.14 = (bf16[2,512,256]{2,1,0:T(8,128)(2,1)S(1)}, bf16[2,512,256]{2,1,0:T(8,128)(2,1)S(1)}, u32[]{:S(2)}, u32[]{:S(2)}) collective-permute-start(bf16[2,512,256]{2,1,0:T(8,128)(2,1)S(1)} %pad_maximum_fusion.3), channel_id=1, source_target_pairs={{0,4},{1,5},{2,6},{3,7},{4,0},{5,1},{6,2},{7,3},{8,12},{9,13},{10,... | collective-permute-start | bytes 1572872 | tf_op jit(solution)/shard_map/ppermute | solution.py:363
  48.0 14.1 %collective-permute-start.20 = (bf16[256,1024]{1,0:T(8,128)(2,1)S(1)}, bf16[256,1024]{1,0:T(8,128)(2,1)S(1)}, u32[]{:S(2)}, u32[]{:S(2)}) collective-permute-start(bf16[256,1024]{1,0:T(8,128)(2,1)S(1)} %get-tuple-element.79), channel_id=1, source_target_pairs={{0,4},{1,5},{2,6},{3,7},{4,0},{5,1},{6,2},{7,3},{8,12},{9,13},{10,... | collective-permute-start | bytes 1572872 | tf_op jit(solution)/shard_map/ppermute | solution.py:363
  48.8 14.9 %collective-permute-start.17 = (bf16[256,1024]{1,0:T(8,128)(2,1)S(1)}, bf16[256,1024]{1,0:T(8,128)(2,1)S(1)}, u32[]{:S(2)}, u32[]{:S(2)}) collective-permute-start(bf16[256,1024]{1,0:T(8,128)(2,1)S(1)} %get-tuple-element.75), channel_id=1, source_target_pairs={{0,2},{1,3},{2,0},{3,1},{4,6},{5,7},{6,4},{7,5},{8,10},{9,11},{10,... | collective-permute-start | bytes 1572872 | tf_op jit(solution)/shard_map/ppermute | solution.py:363
  50.1 12.0 %copy-start.21 = (bf16[2,512,256]{2,1,0:T(8,128)(2,1)S(1)}, bf16[2,512,256]{2,1,0:T(8,128)(2,1)}, u32[]{:S(2)}) copy-start(bf16[2,512,256]{2,1,0:T(8,128)(2,1)} %get-tuple-element.80.refs_4_) | copy-start | bytes 1572868
  50.1 13.7 %copy-start.20 = (bf16[2,512,256]{2,1,0:T(8,128)(2,1)S(1)}, bf16[2,512,256]{2,1,0:T(8,128)(2,1)}, u32[]{:S(2)}) copy-start(bf16[2,512,256]{2,1,0:T(8,128)(2,1)} %get-tuple-element.76.refs_0_) | copy-start | bytes 1572868
  61.4 10.5 %collective-permute-start.16 = (bf16[1,2,256,256]{3,2,1,0:T(8,128)(2,1)S(1)}, bf16[1,2,256,256]{3,2,1,0:T(8,128)(2,1)S(1)}, u32[]{:S(2)}, u32[]{:S(2)}) collective-permute-start(bf16[1,2,256,256]{3,2,1,0:T(8,128)(2,1)S(1)} %dynamic-slice_bitcast_fusion.4), channel_id=1, source_target_pairs={{24,16},{25,17},{26,18},{27,19},{28,20},{29,21},{30,22},{31,23}} | collective-permute-start | bytes 786440 | tf_op jit(solution)/shard_map/ppermute | solution.py:475
  62.1 11.0 %collective-permute-start.21 = (bf16[2,512,256]{2,1,0:T(8,128)(2,1)S(1)}, bf16[2,512,256]{2,1,0:T(8,128)(2,1)S(1)}, u32[]{:S(2)}, u32[]{:S(2)}) collective-permute-start(bf16[2,512,256]{2,1,0:T(8,128)(2,1)S(1)} %copy-done.21), channel_id=1, source_target_pairs={{0,4},{1,5},{2,6},{3,7},{4,0},{5,1},{6,2},{7,3},{8,12},{9,13},{10,... | collective-permute-start | bytes 1572872 | tf_op jit(solution)/shard_map/ppermute | solution.py:363
  63.7 10.1 %collective-permute-start.18 = (bf16[2,512,256]{2,1,0:T(8,128)(2,1)S(1)}, bf16[2,512,256]{2,1,0:T(8,128)(2,1)S(1)}, u32[]{:S(2)}, u32[]{:S(2)}) collective-permute-start(bf16[2,512,256]{2,1,0:T(8,128)(2,1)S(1)} %copy-done.20), channel_id=1, source_target_pairs={{0,2},{1,3},{2,0},{3,1},{4,6},{5,7},{6,4},{7,5},{8,10},{9,11},{10,... | collective-permute-start | bytes 1572872 | tf_op jit(solution)/shard_map/ppermute | solution.py:363
  64.3 9.6 %collective-permute-start.22 = (bf16[256,1024]{1,0:T(8,128)(2,1)S(1)}, bf16[256,1024]{1,0:T(8,128)(2,1)S(1)}, u32[]{:S(2)}, u32[]{:S(2)}) collective-permute-start(bf16[256,1024]{1,0:T(8,128)(2,1)S(1)} %collective-permute-done.20.refs_6_), channel_id=1, source_target_pairs={{0,1},{1,0},{2,3},{3,2},{4,5},{5,4},{6,7},{7,6},{8,9},{9,8},{10,11... | collective-permute-start | bytes 1572872 | tf_op jit(solution)/shard_map/ppermute | solution.py:360
  64.3 9.6 %collective-permute-start.19 = (bf16[256,1024]{1,0:T(8,128)(2,1)S(1)}, bf16[256,1024]{1,0:T(8,128)(2,1)S(1)}, u32[]{:S(2)}, u32[]{:S(2)}) collective-permute-start(bf16[256,1024]{1,0:T(8,128)(2,1)S(1)} %collective-permute-done.17.refs_2_), channel_id=1, source_target_pairs={{0,1},{1,0},{2,3},{3,2},{4,5},{5,4},{6,7},{7,6},{8,9},{9,8},{10,11... | collective-permute-start | bytes 1572872 | tf_op jit(solution)/shard_map/ppermute | solution.py:360
  72.1 19.3 %collective-permute-start.25 = (bf16[2,2,256,256]{3,2,1,0:T(8,128)(2,1)S(1)}, bf16[2,2,256,256]{3,2,1,0:T(8,128)(2,1)S(1)}, u32[]{:S(2)}, u32[]{:S(2)}) collective-permute-start(bf16[2,2,256,256]{3,2,1,0:T(8,128)(2,1)S(1)} %pad_maximum_fusion.5), channel_id=1, source_target_pairs={{16,8},{24,16},{17,9},{25,17},{18,10},{26,18},{19,11},{27,19},{20,... | collective-permute-start | bytes 1572872 | tf_op jit(solution)/shard_map/ppermute | solution.py:475
  81.6 11.3 %collective-permute-start.29 = (bf16[512,256]{1,0:T(8,128)(2,1)}, bf16[512,256]{1,0:T(8,128)(2,1)S(1)}, u32[]{:S(2)}, u32[]{:S(2)}) collective-permute-start(bf16[512,256]{1,0:T(8,128)(2,1)} %get-tuple-element.90), channel_id=1, source_target_pairs={{0,4},{1,5},{2,6},{3,7},{4,0},{5,1},{6,2},{7,3},{8,12},{9,13},{10,... | collective-permute-start | bytes 786440 | tf_op jit(solution)/shard_map/ppermute | solution.py:363
  82.1 11.3 %collective-permute-start.30 = (bf16[512,256]{1,0:T(8,128)(2,1)}, bf16[512,256]{1,0:T(8,128)(2,1)S(1)}, u32[]{:S(2)}, u32[]{:S(2)}) collective-permute-start(bf16[512,256]{1,0:T(8,128)(2,1)} %get-tuple-element.93), channel_id=1, source_target_pairs={{0,2},{1,3},{2,0},{3,1},{4,6},{5,7},{6,4},{7,5},{8,10},{9,11},{10,... | collective-permute-start | bytes 786440 | tf_op jit(solution)/shard_map/ppermute | solution.py:363
  83.1 11.6 %collective-permute-start.33 = (bf16[512,256]{1,0:T(8,128)(2,1)}, bf16[512,256]{1,0:T(8,128)(2,1)S(1)}, u32[]{:S(2)}, u32[]{:S(2)}) collective-permute-start(bf16[512,256]{1,0:T(8,128)(2,1)} %get-tuple-element.100), channel_id=1, source_target_pairs={{0,3},{1,2},{2,1},{3,0},{4,7},{5,6},{6,5},{7,4},{8,11},{9,10},{10,... | collective-permute-start | bytes 786440 | tf_op jit(solution)/shard_map/ppermute | solution.py:516
  90.2 9.7 %collective-permute-start.31 = (bf16[1024,256]{1,0:T(8,128)(2,1)S(1)}, bf16[1024,256]{1,0:T(8,128)(2,1)S(1)}, u32[]{:S(2)}, u32[]{:S(2)}) collective-permute-start(bf16[1024,256]{1,0:T(8,128)(2,1)S(1)} %pad_maximum_fusion.7), channel_id=1, source_target_pairs={{0,1},{1,0},{2,3},{3,2},{4,5},{5,4},{6,7},{7,6},{8,9},{9,8},{10,11... | collective-permute-start | bytes 1572872 | tf_op jit(solution)/shard_map/ppermute | solution.py:360
  91.4 8.3 %collective-permute-start.32 = (bf16[512,256]{1,0:T(8,128)(2,1)S(1)}, bf16[512,256]{1,0:T(8,128)(2,1)S(1)}, u32[]{:S(2)}, u32[]{:S(2)}) collective-permute-start(bf16[512,256]{1,0:T(8,128)(2,1)S(1)} %copy-done.31), channel_id=1, source_target_pairs={{0,5},{1,4},{2,7},{3,6},{4,1},{5,0},{6,3},{7,2},{8,13},{9,12},{10,... | collective-permute-start | bytes 786440 | tf_op jit(solution)/shard_map/ppermute | solution.py:516
  92.9 57.9 %collective-permute-start.23 = (bf16[256,2048]{1,0:T(8,128)(2,1)S(1)}, bf16[256,2048]{1,0:T(8,128)(2,1)S(1)}, u32[]{:S(2)}, u32[]{:S(2)}) collective-permute-start(bf16[256,2048]{1,0:T(8,128)(2,1)S(1)} %copy-done.14), channel_id=1, source_target_pairs={{0,1},{1,0},{2,3},{3,2},{4,5},{5,4},{6,7},{7,6},{8,9},{9,8},{10,11... | collective-permute-start | bytes 3145736 | tf_op jit(solution)/shard_map/ppermute | solution.py:360
  93.4 21.4 %collective-permute-start.26 = (bf16[2,2,256,256]{3,2,1,0:T(8,128)(2,1)S(1)}, bf16[2,2,256,256]{3,2,1,0:T(8,128)(2,1)S(1)}, u32[]{:S(2)}, u32[]{:S(2)}) collective-permute-start(bf16[2,2,256,256]{3,2,1,0:T(8,128)(2,1)S(1)} %pad_maximum_fusion.6), channel_id=1, source_target_pairs={{8,0},{16,8},{24,16},{9,1},{17,9},{25,17},{10,2},{18,10},{26,18},{... | collective-permute-start | bytes 1572872 | tf_op jit(solution)/shard_map/ppermute | solution.py:475
  94.7 21.6 %collective-permute-start.24 = (bf16[256,1024]{1,0:T(8,128)(2,1)S(1)}, bf16[256,1024]{1,0:T(8,128)(2,1)S(1)}, u32[]{:S(2)}, u32[]{:S(2)}) collective-permute-start(bf16[256,1024]{1,0:T(8,128)(2,1)S(1)} %copy-done.17), channel_id=1, source_target_pairs={{0,1},{1,0},{2,3},{3,2},{4,5},{5,4},{6,7},{7,6},{8,9},{9,8},{10,11... | collective-permute-start | bytes 1572872 | tf_op jit(solution)/shard_map/ppermute | solution.py:360
  100.1 16.2 %copy-start.4 = (bf16[256,1024]{1,0:T(8,128)(2,1)S(1)}, bf16[256,1024]{1,0:T(8,128)(2,1)}, u32[]{:S(2)}) copy-start(bf16[256,1024]{1,0:T(8,128)(2,1)} %get-tuple-element.86) | copy-start | bytes 1572868
  100.2 17.5 %collective-permute-start.34 = (bf16[512,256]{1,0:T(8,128)(2,1)S(1)}, bf16[512,256]{1,0:T(8,128)(2,1)S(1)}, u32[]{:S(2)}, u32[]{:S(2)}) collective-permute-start(bf16[512,256]{1,0:T(8,128)(2,1)S(1)} %get-tuple-element.114), channel_id=1, source_target_pairs={{24,16},{25,17},{26,18},{27,19},{28,20},{29,21},{30,22},{31,23}} | collective-permute-start | bytes 786440 | tf_op jit(solution)/shard_map/ppermute | solution.py:451
  101.0 16.7 %collective-permute-start.35 = (bf16[512,256]{1,0:T(8,128)(2,1)S(1)}, bf16[512,256]{1,0:T(8,128)(2,1)S(1)}, u32[]{:S(2)}, u32[]{:S(2)}) collective-permute-start(bf16[512,256]{1,0:T(8,128)(2,1)S(1)} %get-tuple-element.113), channel_id=1, source_target_pairs={{0,8},{1,9},{2,10},{3,11},{4,12},{5,13},{6,14},{7,15}} | collective-permute-start | bytes 786440 | tf_op jit(solution)/shard_map/ppermute | solution.py:451
  114.9 18.4 %collective-permute-start.27 = (bf16[1,2,256,256]{3,2,1,0:T(8,128)(2,1)S(1)}, bf16[1,2,256,256]{3,2,1,0:T(8,128)(2,1)S(1)}, u32[]{:S(2)}, u32[]{:S(2)}) collective-permute-start(bf16[1,2,256,256]{3,2,1,0:T(8,128)(2,1)S(1)} %get-tuple-element.124), channel_id=1, source_target_pairs={{8,0},{16,8},{24,16},{9,1},{17,9},{25,17},{10,2},{18,10},{26,18},{... | collective-permute-start | bytes 786440 | tf_op jit(solution)/shard_map/ppermute | solution.py:475
  116.2 17.2 %collective-permute-start.28 = (bf16[2,256,256]{2,1,0:T(8,128)(2,1)S(1)}, bf16[2,256,256]{2,1,0:T(8,128)(2,1)S(1)}, u32[]{:S(2)}, u32[]{:S(2)}) collective-permute-start(bf16[2,256,256]{2,1,0:T(8,128)(2,1)S(1)} %get-tuple-element.125), channel_id=1, source_target_pairs={{0,1},{1,0},{2,3},{3,2},{4,5},{5,4},{6,7},{7,6},{8,9},{9,8},{10,11... | collective-permute-start | bytes 786440 | tf_op jit(solution)/shard_map/ppermute | solution.py:360
  117.9 16.5 %collective-permute-start.36 = (bf16[512,256]{1,0:T(8,128)(2,1)S(1)}, bf16[512,256]{1,0:T(8,128)(2,1)S(1)}, u32[]{:S(2)}, u32[]{:S(2)}) collective-permute-start(bf16[512,256]{1,0:T(8,128)(2,1)S(1)} %get-tuple-element.112), channel_id=1, source_target_pairs={{16,8},{24,16},{17,9},{25,17},{18,10},{26,18},{19,11},{27,19},{20,... | collective-permute-start | bytes 786440 | tf_op jit(solution)/shard_map/ppermute | solution.py:451
  118.5 32.3 %copy-start = (f32[256,2048]{1,0:T(8,128)S(1)}, f32[256,2048]{1,0:T(8,128)}, u32[]{:S(2)}) copy-start(f32[256,2048]{1,0:T(8,128)} %get-tuple-element.84) | copy-start | bytes 6291460
  118.5 20.0 %collective-permute-start.37 = (bf16[512,256]{1,0:T(8,128)(2,1)S(1)}, bf16[512,256]{1,0:T(8,128)(2,1)S(1)}, u32[]{:S(2)}, u32[]{:S(2)}) collective-permute-start(bf16[512,256]{1,0:T(8,128)(2,1)S(1)} %get-tuple-element.111), channel_id=1, source_target_pairs={{0,8},{8,16},{1,9},{9,17},{2,10},{10,18},{3,11},{11,19},{4,12},{12... | collective-permute-start | bytes 786440 | tf_op jit(solution)/shard_map/ppermute | solution.py:451
  138.7 14.7 %collective-permute-start.38 = (bf16[512,256]{1,0:T(8,128)(2,1)S(1)}, bf16[512,256]{1,0:T(8,128)(2,1)S(1)}, u32[]{:S(2)}, u32[]{:S(2)}) collective-permute-start(bf16[512,256]{1,0:T(8,128)(2,1)S(1)} %get-tuple-element.110), channel_id=1, source_target_pairs={{8,0},{16,8},{24,16},{9,1},{17,9},{25,17},{10,2},{18,10},{26,18},{... | collective-permute-start | bytes 786440 | tf_op jit(solution)/shard_map/ppermute | solution.py:451
  140.0 14.6 %collective-permute-start.39 = (bf16[512,256]{1,0:T(8,128)(2,1)S(1)}, bf16[512,256]{1,0:T(8,128)(2,1)S(1)}, u32[]{:S(2)}, u32[]{:S(2)}) collective-permute-start(bf16[512,256]{1,0:T(8,128)(2,1)S(1)} %get-tuple-element.109), channel_id=1, source_target_pairs={{0,8},{8,16},{16,24},{1,9},{9,17},{17,25},{2,10},{10,18},{18,26},{... | collective-permute-start | bytes 786440 | tf_op jit(solution)/shard_map/ppermute | solution.py:451
  (26 other events, 118.4 us)

commit v2 on v1

--- a/solution.py
+++ b/solution.py
@@ -64,9 +64,9 @@
     key = lax.broadcasted_iota(jnp.int32, (BLOCK_SIZE, STACK), 0)
     query = lax.broadcasted_iota(jnp.int32, (BLOCK_SIZE, STACK), 1) & (BLOCK_SIZE - 1)
     parts = [jnp.where(key <= query, s_t[:BLOCK_SIZE], NEG)]
-    for j in range(1, slots):
-        parts.append(jnp.where(j < count, s_t[j * BLOCK_SIZE:(j + 1) * BLOCK_SIZE], NEG))
-    return jnp.concatenate(parts, axis=0)
+    parts.append(s_t[BLOCK_SIZE:(slots - 1) * BLOCK_SIZE])
+    parts.append(jnp.where(slots <= count, s_t[(slots - 1) * BLOCK_SIZE:], NEG))
+    return jnp.concatenate([part for part in parts if part.shape[0]], axis=0)
 
 
 def by_count(count, run):

time: 154 us -> 155 us (level)
  no operation moved by 1% of the time
where the time goes in v2:
time: 155 us
  starting transfers between devices  70 us (45%)
  Pallas kernels  39.8 us (26%)
  waiting for transfers between devices  25.1 us (16%)
  local copies, waits for them, and re-layouts  11.3 us (7%)
  other arithmetic  7.45 us (5%)
    ppermute x6, starting transfers between devices, send(): self.got = lax.ppermute(self.sent, 'ctx', pairs)  36.5 us
    pallas_call x2, Pallas kernels, backward(): pl.pallas_call(functools.partial(backward_kernel, nc, nb, plan, width), g...  16.5 us
    ppermute x12, starting transfers between devices, to_chip(): return lax.ppermute(x, 'fsdp', [(p, p ^ 2 * bit) for p in range(nf)])  13.6 us
    ppermute x6, starting transfers between devices, hop_up(): return lax.ppermute(x, 'ctx', [(p, p + 1) for p in range(step - 1, nc - 1)])  10.4 us
    pallas_call x1, Pallas kernels, forward(): pl.pallas_call(functools.partial(forward_kernel, nc, nb), grid_spec=pltpu...  7.5 us
    pallas_call x1, Pallas kernels, mix(): pl.pallas_call(functools.partial(mix_kernel, plan, width), in_specs=[pl.B...  7.01 us
    ppermute x6, waiting for transfers between devices, send(): self.got = lax.ppermute(self.sent, 'ctx', pairs)  6.77 us
    ppermute x12, waiting for transfers between devices, to_chip(): return lax.ppermute(x, 'fsdp', [(p, p ^ 2 * bit) for p in range(nf)])  6.38 us
  transfers between devices with their start and end apart: 40, of which 11 were waited for; matrix products, arithmetic and copies ran while one was open for 7% of the time, Pallas kernels for 26%

profile of v2, /device:TPU:0, one launch (start us, length us, event | category | flops | bytes accessed | tf_op | source)
XLA Modules:
  0.0 155.0 jit_solution(1415353212858165963)
XLA Ops:
  0.7 1.4 constant_dynamic-slice_fusion.2
  2.1 3.0 %collective-permute-start.11 = (bf16[1024,256]{1,0:T(8,128)(2,1)S(1)}, bf16[1024,256]{1,0:T(8,128)(2,1)}, u32[]{:S(2)}, u32[]{:S(2)}) collective-permute-start(bf16[1024,256]{1,0:T(8,128)(2,1)S(1)} %get-tuple-element.118.rest_6_.rest_0_), channel_id=1, source_target_pairs={{0,4},{1,5},{2,6},{3,7},{4,0},{5,1},{6,2},{7,3},{8,12},{9,13},{10,... | collective-permute-start | bytes 1572872 | tf_op jit(solution)/shard_map/ppermute | solution.py:363
  5.1 1.5 collective-permute-start.10
  8.0 4.2 %collective-permute-start = (bf16[256,512]{1,0:T(8,128)(2,1)}, bf16[256,512]{1,0:T(8,128)(2,1)}, u32[]{:S(2)}, u32[]{:S(2)}) collective-permute-start(bf16[256,512]{1,0:T(8,128)(2,1)} %pad_maximum_fusion.8.rest_0_), channel_id=1, source_target_pairs={{0,8},{8,16},{16,24},{1,9},{9,17},{17,25},{2,10},{10,18},{18,26},{... | collective-permute-start | bytes 786440 | tf_op jit(solution)/shard_map/ppermute | solution.py:377
  13.5 3.5 %collective-permute-start.3 = (bf16[256,512]{1,0:T(8,128)(2,1)}, bf16[256,512]{1,0:T(8,128)(2,1)}, u32[]{:S(2)}, u32[]{:S(2)}) collective-permute-start(bf16[256,512]{1,0:T(8,128)(2,1)} %copy-done.28), channel_id=1, source_target_pairs={{0,8},{8,16},{16,24},{1,9},{9,17},{17,25},{2,10},{10,18},{18,26},{... | collective-permute-start | bytes 786440 | tf_op jit(solution)/shard_map/ppermute | solution.py:377
  21.0 2.1 %collective-permute-done.3.rest_5_.rest_1_ = bf16[256,512]{1,0:T(8,128)(2,1)} collective-permute-done((bf16[256,512]{1,0:T(8,128)(2,1)}, bf16[256,512]{1,0:T(8,128)(2,1)}, u32[]{:S(2)}, u32[]{:S(2)}) %collective-permute-start.3) | collective-permute-done | bytes 262176 | tf_op jit(solution)/shard_map/ppermute | solution.py:377
  23.9 1.0 slice_bitcast_fusion.3
  25.6 1.0 slice_bitcast_fusion.5
  27.2 4.8 %collective-permute-done.13.rest_11_.rest_5_ = bf16[1024,256]{1,0:T(8,128)(2,1)S(1)} collective-permute-done((bf16[1024,256]{1,0:T(8,128)(2,1)}, bf16[1024,256]{1,0:T(8,128)(2,1)S(1)}, u32[]{:S(2)}, u32[]{:S(2)}) %collective-permute-start.13) | collective-permute-done | bytes 524320 | tf_op jit(solution)/shard_map/ppermute | solution.py:363
  32.9 0.8 collective-permute-start.15
  33.8 1.3 collective-permute-start.14
  35.1 1.0 copy-done.15
  36.1 2.9 %halve.1.q_ref = bf16[2,256,1024]{2,1,0:T(8,128)(2,1)} custom-call(s32[3]{0:T(128)} %pad_add_fusion.3.meta_ref, bf16[256,2048]{1,0:T(8,128)(2,1)} %bitcast.104, bf16[256,2048]{1,0:T(8,128)(2,1)} %copy-done.15), custom_call_target="tpu_custom_call" | custom-call | flops 20000000000 | bytes 1000000 | tf_op jit(solution)/shard_map/halve/pallas_call | solution.py:328
  40.4 7.5 %attention_forward.1 = (bf16[2,256,1024]{2,1,0:T(8,128)(2,1)}, bf16[2,512,256]{2,1,0:T(8,128)(2,1)}, bf16[2,512,256]{2,1,0:T(8,128)(2,1)}, f32[4,2,1,512]{3,2,1,0:T(1,128)}) custom-call(s32[2,8]{1,0:T(2,128)} %bl_ref.5, s32[2]{0:T(128)} %bc_ref.5, s32[3]{0:T(128)} %pad_add_fusion.3.meta_ref, bf16[2,256,1024]{2,1,0:T(8,128)(2,1)} %halve.1.q_ref, ...), custom_call_target="tpu_custom_call" | custom-call | flops 20000000000 | bytes 1000000 | tf_op jit(solution)/shard_map/attention_forward/pallas_call | solution.py:131
  48.0 0.8 collective-permute-start.20
  48.8 1.2 collective-permute-start.17
  50.1 10.3 %attention_backward.2 = (bf16[256,1024]{1,0:T(8,128)(2,1)}, bf16[2,1024,256]{2,1,0:T(8,128)(2,1)}, bf16[256,1024]{1,0:T(8,128)(2,1)}) custom-call(s32[2,8]{1,0:T(2,128)} %bl_ref.5, s32[2]{0:T(128)} %bc_ref.5, s32[3]{0:T(128)} %pad_add_fusion.3.meta_ref, bf16[2,256,1024]{2,1,0:T(8,128)(2,1)} %halve.1.q_ref, bf16[2,256,1024]{2,1,0:T(8,128)(2,1)} %get-tuple-element.83.a_ref, ...), custom_call_target="tpu_custom_call" | custom-call | flops 20000000000 | bytes 1000000 | tf_op jit(solution)/shard_map/attention_backward/pallas_call | solution.py:212
  60.4 1.0 dynamic-slice_bitcast_fusion.4
  62.1 1.6 %collective-permute-start.21 = (bf16[2,512,256]{2,1,0:T(8,128)(2,1)S(1)}, bf16[2,512,256]{2,1,0:T(8,128)(2,1)S(1)}, u32[]{:S(2)}, u32[]{:S(2)}) collective-permute-start(bf16[2,512,256]{2,1,0:T(8,128)(2,1)S(1)} %copy-done.21), channel_id=1, source_target_pairs={{0,4},{1,5},{2,6},{3,7},{4,0},{5,1},{6,2},{7,3},{8,12},{9,13},{10,... | collective-permute-start | bytes 1572872 | tf_op jit(solution)/shard_map/ppermute | solution.py:363
  64.8 6.1 %attention_backward.3 = (bf16[256,1024]{1,0:T(8,128)(2,1)}, bf16[2,1024,256]{2,1,0:T(8,128)(2,1)}) custom-call(s32[2,8]{1,0:T(2,128)} %bl_ref.5, s32[2]{0:T(128)} %bc_ref.5, s32[3]{0:T(128)} %pad_add_fusion.3.meta_ref, bf16[2,256,1024]{2,1,0:T(8,128)(2,1)} %halve.1.q_ref, bf16[2,256,1024]{2,1,0:T(8,128)(2,1)} %get-tuple-element.83.a_ref, ...), custom_call_target="tpu_custom_call" | custom-call | flops 20000000000 | bytes 1000000 | tf_op jit(solution)/shard_map/attention_backward/pallas_call | solution.py:212
  71.0 1.0 dynamic-slice_bitcast_fusion.3
  72.1 1.0 collective-permute-start.25
  73.1 0.8 collective-permute-done.18.refs_1_
  73.9 0.8 copy-done.25
  74.8 0.8 copy-done.27
  75.6 5.9 %proj_parts.1 = (bf16[512,256]{1,0:T(8,128)(2,1)}, bf16[512,256]{1,0:T(8,128)(2,1)}, bf16[512,256]{1,0:T(8,128)(2,1)}, bf16[512,256]{1,0:T(8,128)(2,1)}, bf16[51...) custom-call(s32[2,2,2,2]{3,2,1,0:T(2,128)} %pad_add_fusion.cols_ref, ...), custom_call_target="tpu_custom_call" | custom-call | flops 20000000000 | bytes 1000000 | tf_op jit(solution)/shard_map/proj_parts/pallas_call | solution.py:309
  82.1 1.0 collective-permute-start.30
  83.1 7.0 %mix.1 = (f32[256,2048]{1,0:T(8,128)}, bf16[256,2048]{1,0:T(8,128)(2,1)}) custom-call(s32[3]{0:T(128)} %pad_add_fusion.3.meta_ref, bf16[2,256,1024]{2,1,0:T(8,128)(2,1)} %get-tuple-element.83.a_ref, bf16[256,2048]{1,0:T(8,128)(2,1)} %bitcast.105, bf16[1024,256]{1,0:T(8,128)(2,1)} %copy-done.5, bf16[1024,256]{1,0:T(8,128)(2,1)} %copy-done.16, ...), custom_call_target="tpu_custom_call" | custom-call | flops 20000000000 | bytes 1000000 | tf_op jit(solution)/shard_map/mix/pallas_call | solution.py:281
  90.2 1.2 collective-permute-start.31
  91.4 1.2 collective-permute-start.32
  93.4 1.3 collective-permute-start.26
  94.7 1.0 collective-permute-start.24
  95.6 4.1 %collective-permute-done.32 = bf16[512,256]{1,0:T(8,128)(2,1)S(1)} collective-permute-done((bf16[512,256]{1,0:T(8,128)(2,1)S(1)}, bf16[512,256]{1,0:T(8,128)(2,1)S(1)}, u32[]{:S(2)}, u32[]{:S(2)}) %collective-permute-start.32) | collective-permute-done | bytes 262176 | tf_op jit(solution)/shard_map/ppermute | solution.py:516
  100.2 0.8 collective-permute-start.34
  101.0 12.6 %collective-permute-start.35 = (bf16[512,256]{1,0:T(8,128)(2,1)S(1)}, bf16[512,256]{1,0:T(8,128)(2,1)S(1)}, u32[]{:S(2)}, u32[]{:S(2)}) collective-permute-start(bf16[512,256]{1,0:T(8,128)(2,1)S(1)} %get-tuple-element.113), channel_id=1, source_target_pairs={{0,8},{1,9},{2,10},{3,11},{4,12},{5,13},{6,14},{7,15}} | collective-permute-start | bytes 786440 | tf_op jit(solution)/shard_map/ppermute | solution.py:451
  113.7 4.0 %collective-permute-done.26 = bf16[2,2,256,256]{3,2,1,0:T(8,128)(2,1)S(1)} collective-permute-done((bf16[2,2,256,256]{3,2,1,0:T(8,128)(2,1)S(1)}, bf16[2,2,256,256]{3,2,1,0:T(8,128)(2,1)S(1)}, u32[]{:S(2)}, u32[]{:S(2)}) %collective-permute-start.26) | collective-permute-done | bytes 524320 | tf_op jit(solution)/shard_map/ppermute | solution.py:475
  117.9 1.3 collective-permute-start.27
  119.3 1.4 maximum_select_fusion
  121.5 10.4 %collective-permute-start.37 = (bf16[512,256]{1,0:T(8,128)(2,1)S(1)}, bf16[512,256]{1,0:T(8,128)(2,1)S(1)}, u32[]{:S(2)}, u32[]{:S(2)}) collective-permute-start(bf16[512,256]{1,0:T(8,128)(2,1)S(1)} %get-tuple-element.111), channel_id=1, source_target_pairs={{0,8},{8,16},{1,9},{9,17},{2,10},{10,18},{3,11},{11,19},{4,12},{12... | collective-permute-start | bytes 786440 | tf_op jit(solution)/shard_map/ppermute | solution.py:451
  131.9 0.9 collective-permute-done.27
  133.1 0.8 fusion.13
  133.9 4.2 %collective-permute-done.37 = bf16[512,256]{1,0:T(8,128)(2,1)S(1)} collective-permute-done((bf16[512,256]{1,0:T(8,128)(2,1)S(1)}, bf16[512,256]{1,0:T(8,128)(2,1)S(1)}, u32[]{:S(2)}, u32[]{:S(2)}) %collective-permute-start.37) | collective-permute-done | bytes 262176 | tf_op jit(solution)/shard_map/ppermute | solution.py:451
  138.2 1.3 collective-permute-start.38
  139.5 10.7 %collective-permute-start.39 = (bf16[512,256]{1,0:T(8,128)(2,1)S(1)}, bf16[512,256]{1,0:T(8,128)(2,1)S(1)}, u32[]{:S(2)}, u32[]{:S(2)}) collective-permute-start(bf16[512,256]{1,0:T(8,128)(2,1)S(1)} %get-tuple-element.109), channel_id=1, source_target_pairs={{0,8},{8,16},{16,24},{1,9},{9,17},{17,25},{2,10},{10,18},{18,26},{... | collective-permute-start | bytes 786440 | tf_op jit(solution)/shard_map/ppermute | solution.py:451
  150.3 1.3 fusion
  151.6 1.3 collective-permute-done.38
  152.9 1.2 collective-permute-done.39
  154.1 0.9 convert_add_fusion.6
  (149 shorter events, 16.2 us)
Async XLA Ops:
  0.7 11.7 %copy-start.3 = (bf16[1,256,2048]{2,1,0:T(8,128)(2,1)S(1)}, bf16[1,256,2048]{2,1,0:T(8,128)(2,1)}, u32[]{:S(2)}) copy-start(bf16[1,256,2048]{2,1,0:T(8,128)(2,1)} %param.12) | copy-start | bytes 3145732
  2.1 15.7 %copy-start.5 = (bf16[1024,256]{1,0:T(8,128)(2,1)}, bf16[1024,256]{1,0:T(8,128)(2,1)S(1)}, u32[]{:S(2)}) copy-start(bf16[1024,256]{1,0:T(8,128)(2,1)S(1)} %get-tuple-element.118.rest_6_.rest_0_) | copy-start | bytes 1572868
  2.1 17.0 %collective-permute-start.11 = (bf16[1024,256]{1,0:T(8,128)(2,1)S(1)}, bf16[1024,256]{1,0:T(8,128)(2,1)}, u32[]{:S(2)}, u32[]{:S(2)}) collective-permute-start(bf16[1024,256]{1,0:T(8,128)(2,1)S(1)} %get-tuple-element.118.rest_6_.rest_0_), channel_id=1, source_target_pairs={{0,4},{1,5},{2,6},{3,7},{4,0},{5,1},{6,2},{7,3},{8,12},{9,13},{10,... | collective-permute-start | bytes 1572872 | tf_op jit(solution)/shard_map/ppermute | solution.py:363
  5.1 15.2 %collective-permute-start.10 = (bf16[1024,256]{1,0:T(8,128)(2,1)S(1)}, bf16[1024,256]{1,0:T(8,128)(2,1)}, u32[]{:S(2)}, u32[]{:S(2)}) collective-permute-start(bf16[1024,256]{1,0:T(8,128)(2,1)S(1)} %get-tuple-element.118.rest_6_.rest_0_), channel_id=1, source_target_pairs={{0,2},{1,3},{2,0},{3,1},{4,6},{5,7},{6,4},{7,5},{8,10},{9,11},{10,... | collective-permute-start | bytes 1572872 | tf_op jit(solution)/shard_map/ppermute | solution.py:363
  6.6 5.8 %collective-permute-start.5 = (bf16[1024,256]{1,0:T(8,128)(2,1)S(1)}, bf16[1024,256]{1,0:T(8,128)(2,1)S(1)}, u32[]{:S(2)}, u32[]{:S(2)}) collective-permute-start(bf16[1024,256]{1,0:T(8,128)(2,1)S(1)} %get-tuple-element.119), channel_id=1, source_target_pairs={{0,1},{1,0},{2,3},{3,2},{4,5},{5,4},{6,7},{7,6},{8,9},{9,8},{10,11... | collective-permute-start | bytes 1572872 | tf_op jit(solution)/shard_map/ppermute | solution.py:360
  6.7 5.7 %collective-permute-start.2 = (bf16[256,512]{1,0:T(8,128)(2,1)S(1)}, bf16[256,512]{1,0:T(8,128)(2,1)S(1)}, u32[]{:S(2)}, u32[]{:S(2)}) collective-permute-start(bf16[256,512]{1,0:T(8,128)(2,1)S(1)} %pad_maximum_fusion.9), channel_id=1, source_target_pairs={{0,1},{1,0},{2,3},{3,2},{4,5},{5,4},{6,7},{7,6},{8,9},{9,8},{10,11... | collective-permute-start | bytes 786440 | tf_op jit(solution)/shard_map/ppermute | solution.py:360
  8.0 10.5 %collective-permute-start = (bf16[256,512]{1,0:T(8,128)(2,1)}, bf16[256,512]{1,0:T(8,128)(2,1)}, u32[]{:S(2)}, u32[]{:S(2)}) collective-permute-start(bf16[256,512]{1,0:T(8,128)(2,1)} %pad_maximum_fusion.8.rest_0_), channel_id=1, source_target_pairs={{0,8},{8,16},{16,24},{1,9},{9,17},{17,25},{2,10},{10,18},{18,26},{... | collective-permute-start | bytes 786440 | tf_op jit(solution)/shard_map/ppermute | solution.py:377
  12.4 11.4 %collective-permute-start.6 = (bf16[256,2048]{1,0:T(8,128)(2,1)S(1)}, bf16[256,2048]{1,0:T(8,128)(2,1)}, u32[]{:S(2)}, u32[]{:S(2)}) collective-permute-start(bf16[256,2048]{1,0:T(8,128)(2,1)S(1)} %bitcast.100), channel_id=1, source_target_pairs={{0,1},{1,0},{2,3},{3,2},{4,5},{5,4},{6,7},{7,6},{8,9},{9,8},{10,11... | collective-permute-start | bytes 3145736 | tf_op jit(solution)/shard_map/ppermute | solution.py:360
  13.5 9.6 %collective-permute-start.3 = (bf16[256,512]{1,0:T(8,128)(2,1)}, bf16[256,512]{1,0:T(8,128)(2,1)}, u32[]{:S(2)}, u32[]{:S(2)}) collective-permute-start(bf16[256,512]{1,0:T(8,128)(2,1)} %copy-done.28), channel_id=1, source_target_pairs={{0,8},{8,16},{16,24},{1,9},{9,17},{17,25},{2,10},{10,18},{18,26},{... | collective-permute-start | bytes 786440 | tf_op jit(solution)/shard_map/ppermute | solution.py:377
  18.4 6.4 %collective-permute-start.1 = (bf16[256,512]{1,0:T(8,128)(2,1)}, bf16[256,512]{1,0:T(8,128)(2,1)S(1)}, u32[]{:S(2)}, u32[]{:S(2)}) collective-permute-start(bf16[256,512]{1,0:T(8,128)(2,1)} %collective-permute-done.rest_1_), channel_id=1, source_target_pairs={{8,16},{16,24},{9,17},{17,25},{10,18},{18,26},{11,19},{19,27},{12,... | collective-permute-start | bytes 786440 | tf_op jit(solution)/shard_map/ppermute | solution.py:377
  19.1 13.0 %collective-permute-start.13 = (bf16[1024,256]{1,0:T(8,128)(2,1)}, bf16[1024,256]{1,0:T(8,128)(2,1)S(1)}, u32[]{:S(2)}, u32[]{:S(2)}) collective-permute-start(bf16[1024,256]{1,0:T(8,128)(2,1)} %copy-done.16), channel_id=1, source_target_pairs={{0,4},{1,5},{2,6},{3,7},{4,0},{5,1},{6,2},{7,3},{8,12},{9,13},{10,... | collective-permute-start | bytes 1572872 | tf_op jit(solution)/shard_map/ppermute | solution.py:363
  20.3 12.6 %collective-permute-start.12 = (bf16[1024,256]{1,0:T(8,128)(2,1)}, bf16[1024,256]{1,0:T(8,128)(2,1)S(1)}, u32[]{:S(2)}, u32[]{:S(2)}) collective-permute-start(bf16[1024,256]{1,0:T(8,128)(2,1)} %copy-done.16), channel_id=1, source_target_pairs={{0,2},{1,3},{2,0},{3,1},{4,6},{5,7},{6,4},{7,5},{8,10},{9,11},{10,... | collective-permute-start | bytes 1572872 | tf_op jit(solution)/shard_map/ppermute | solution.py:363
  23.1 3.4 %collective-permute-start.4 = (bf16[256,512]{1,0:T(8,128)(2,1)}, bf16[256,512]{1,0:T(8,128)(2,1)S(1)}, u32[]{:S(2)}, u32[]{:S(2)}) collective-permute-start(bf16[256,512]{1,0:T(8,128)(2,1)} %collective-permute-done.3.rest_5_.rest_1_), channel_id=1, source_target_pairs={{8,16},{16,24},{9,17},{17,25},{10,18},{18,26},{11,19},{19,27},{12,... | collective-permute-start | bytes 786440 | tf_op jit(solution)/shard_map/ppermute | solution.py:377
  23.8 11.3 %collective-permute-start.7 = (bf16[256,2048]{1,0:T(8,128)(2,1)}, bf16[256,2048]{1,0:T(8,128)(2,1)S(1)}, u32[]{:S(2)}, u32[]{:S(2)}) collective-permute-start(bf16[256,2048]{1,0:T(8,128)(2,1)} %bitcast.103), channel_id=1, source_target_pairs={{0,1},{1,0},{2,3},{3,2},{4,5},{5,4},{6,7},{7,6},{8,9},{9,8},{10,11... | collective-permute-start | bytes 3145736 | tf_op jit(solution)/shard_map/ppermute | solution.py:360
  24.9 14.1 %copy-start.29 = (bf16[256,512]{1,0:T(8,128)(2,1)}, bf16[256,512]{1,0:T(8,128)(2,1)S(1)}, u32[]{:S(2)}) copy-start(bf16[256,512]{1,0:T(8,128)(2,1)S(1)} %collective-permute-done.1.rest_2_) | copy-start | bytes 786436
  24.9 14.1 %collective-permute-start.8 = (bf16[256,512]{1,0:T(8,128)(2,1)S(1)}, bf16[256,512]{1,0:T(8,128)(2,1)S(1)}, u32[]{:S(2)}, u32[]{:S(2)}) collective-permute-start(bf16[256,512]{1,0:T(8,128)(2,1)S(1)} %collective-permute-done.1.rest_2_), channel_id=1, source_target_pairs={{16,24},{17,25},{18,26},{19,27},{20,28},{21,29},{22,30},{23,31}} | collective-permute-start | bytes 786440 | tf_op jit(solution)/shard_map/ppermute | solution.py:377
  26.5 12.4 %copy-start.32 = (bf16[256,512]{1,0:T(8,128)(2,1)}, bf16[256,512]{1,0:T(8,128)(2,1)S(1)}, u32[]{:S(2)}) copy-start(bf16[256,512]{1,0:T(8,128)(2,1)S(1)} %collective-permute-done.4.rest_6_.rest_2_) | copy-start | bytes 786436
  26.6 12.5 %collective-permute-start.9 = (bf16[256,512]{1,0:T(8,128)(2,1)S(1)}, bf16[256,512]{1,0:T(8,128)(2,1)S(1)}, u32[]{:S(2)}, u32[]{:S(2)}) collective-permute-start(bf16[256,512]{1,0:T(8,128)(2,1)S(1)} %collective-permute-done.4.rest_6_.rest_2_), channel_id=1, source_target_pairs={{16,24},{17,25},{18,26},{19,27},{20,28},{21,29},{22,30},{23,31}} | collective-permute-start | bytes 786440 | tf_op jit(solution)/shard_map/ppermute | solution.py:377
  32.9 15.0 %collective-permute-start.15 = (bf16[2,512,256]{2,1,0:T(8,128)(2,1)S(1)}, bf16[2,512,256]{2,1,0:T(8,128)(2,1)S(1)}, u32[]{:S(2)}, u32[]{:S(2)}) collective-permute-start(bf16[2,512,256]{2,1,0:T(8,128)(2,1)S(1)} %pad_maximum_fusion.4), channel_id=1, source_target_pairs={{0,2},{1,3},{2,0},{3,1},{4,6},{5,7},{6,4},{7,5},{8,10},{9,11},{10,... | collective-permute-start | bytes 1572872 | tf_op jit(solution)/shard_map/ppermute | solution.py:363
  33.8 14.2 %collective-permute-start.14 = (bf16[2,512,256]{2,1,0:T(8,128)(2,1)S(1)}, bf16[2,512,256]{2,1,0:T(8,128)(2,1)S(1)}, u32[]{:S(2)}, u32[]{:S(2)}) collective-permute-start(bf16[2,512,256]{2,1,0:T(8,128)(2,1)S(1)} %pad_maximum_fusion.3), channel_id=1, source_target_pairs={{0,4},{1,5},{2,6},{3,7},{4,0},{5,1},{6,2},{7,3},{8,12},{9,13},{10,... | collective-permute-start | bytes 1572872 | tf_op jit(solution)/shard_map/ppermute | solution.py:363
  48.0 14.1 %collective-permute-start.20 = (bf16[256,1024]{1,0:T(8,128)(2,1)S(1)}, bf16[256,1024]{1,0:T(8,128)(2,1)S(1)}, u32[]{:S(2)}, u32[]{:S(2)}) collective-permute-start(bf16[256,1024]{1,0:T(8,128)(2,1)S(1)} %get-tuple-element.79), channel_id=1, source_target_pairs={{0,4},{1,5},{2,6},{3,7},{4,0},{5,1},{6,2},{7,3},{8,12},{9,13},{10,... | collective-permute-start | bytes 1572872 | tf_op jit(solution)/shard_map/ppermute | solution.py:363
  48.8 14.9 %collective-permute-start.17 = (bf16[256,1024]{1,0:T(8,128)(2,1)S(1)}, bf16[256,1024]{1,0:T(8,128)(2,1)S(1)}, u32[]{:S(2)}, u32[]{:S(2)}) collective-permute-start(bf16[256,1024]{1,0:T(8,128)(2,1)S(1)} %get-tuple-element.75), channel_id=1, source_target_pairs={{0,2},{1,3},{2,0},{3,1},{4,6},{5,7},{6,4},{7,5},{8,10},{9,11},{10,... | collective-permute-start | bytes 1572872 | tf_op jit(solution)/shard_map/ppermute | solution.py:363
  50.1 12.0 %copy-start.21 = (bf16[2,512,256]{2,1,0:T(8,128)(2,1)S(1)}, bf16[2,512,256]{2,1,0:T(8,128)(2,1)}, u32[]{:S(2)}) copy-start(bf16[2,512,256]{2,1,0:T(8,128)(2,1)} %get-tuple-element.80.refs_4_) | copy-start | bytes 1572868
  50.1 13.7 %copy-start.20 = (bf16[2,512,256]{2,1,0:T(8,128)(2,1)S(1)}, bf16[2,512,256]{2,1,0:T(8,128)(2,1)}, u32[]{:S(2)}) copy-start(bf16[2,512,256]{2,1,0:T(8,128)(2,1)} %get-tuple-element.76.refs_0_) | copy-start | bytes 1572868
  61.4 10.6 %collective-permute-start.16 = (bf16[1,2,256,256]{3,2,1,0:T(8,128)(2,1)S(1)}, bf16[1,2,256,256]{3,2,1,0:T(8,128)(2,1)S(1)}, u32[]{:S(2)}, u32[]{:S(2)}) collective-permute-start(bf16[1,2,256,256]{3,2,1,0:T(8,128)(2,1)S(1)} %dynamic-slice_bitcast_fusion.4), channel_id=1, source_target_pairs={{24,16},{25,17},{26,18},{27,19},{28,20},{29,21},{30,22},{31,23}} | collective-permute-start | bytes 786440 | tf_op jit(solution)/shard_map/ppermute | solution.py:475
  62.1 11.0 %collective-permute-start.21 = (bf16[2,512,256]{2,1,0:T(8,128)(2,1)S(1)}, bf16[2,512,256]{2,1,0:T(8,128)(2,1)S(1)}, u32[]{:S(2)}, u32[]{:S(2)}) collective-permute-start(bf16[2,512,256]{2,1,0:T(8,128)(2,1)S(1)} %copy-done.21), channel_id=1, source_target_pairs={{0,4},{1,5},{2,6},{3,7},{4,0},{5,1},{6,2},{7,3},{8,12},{9,13},{10,... | collective-permute-start | bytes 1572872 | tf_op jit(solution)/shard_map/ppermute | solution.py:363
  63.7 10.1 %collective-permute-start.18 = (bf16[2,512,256]{2,1,0:T(8,128)(2,1)S(1)}, bf16[2,512,256]{2,1,0:T(8,128)(2,1)S(1)}, u32[]{:S(2)}, u32[]{:S(2)}) collective-permute-start(bf16[2,512,256]{2,1,0:T(8,128)(2,1)S(1)} %copy-done.20), channel_id=1, source_target_pairs={{0,2},{1,3},{2,0},{3,1},{4,6},{5,7},{6,4},{7,5},{8,10},{9,11},{10,... | collective-permute-start | bytes 1572872 | tf_op jit(solution)/shard_map/ppermute | solution.py:363
  64.3 9.6 %collective-permute-start.22 = (bf16[256,1024]{1,0:T(8,128)(2,1)S(1)}, bf16[256,1024]{1,0:T(8,128)(2,1)S(1)}, u32[]{:S(2)}, u32[]{:S(2)}) collective-permute-start(bf16[256,1024]{1,0:T(8,128)(2,1)S(1)} %collective-permute-done.20.refs_6_), channel_id=1, source_target_pairs={{0,1},{1,0},{2,3},{3,2},{4,5},{5,4},{6,7},{7,6},{8,9},{9,8},{10,11... | collective-permute-start | bytes 1572872 | tf_op jit(solution)/shard_map/ppermute | solution.py:360
  64.3 9.6 %collective-permute-start.19 = (bf16[256,1024]{1,0:T(8,128)(2,1)S(1)}, bf16[256,1024]{1,0:T(8,128)(2,1)S(1)}, u32[]{:S(2)}, u32[]{:S(2)}) collective-permute-start(bf16[256,1024]{1,0:T(8,128)(2,1)S(1)} %collective-permute-done.17.refs_2_), channel_id=1, source_target_pairs={{0,1},{1,0},{2,3},{3,2},{4,5},{5,4},{6,7},{7,6},{8,9},{9,8},{10,11... | collective-permute-start | bytes 1572872 | tf_op jit(solution)/shard_map/ppermute | solution.py:360
  72.1 19.3 %collective-permute-start.25 = (bf16[2,2,256,256]{3,2,1,0:T(8,128)(2,1)S(1)}, bf16[2,2,256,256]{3,2,1,0:T(8,128)(2,1)S(1)}, u32[]{:S(2)}, u32[]{:S(2)}) collective-permute-start(bf16[2,2,256,256]{3,2,1,0:T(8,128)(2,1)S(1)} %pad_maximum_fusion.5), channel_id=1, source_target_pairs={{16,8},{24,16},{17,9},{25,17},{18,10},{26,18},{19,11},{27,19},{20,... | collective-permute-start | bytes 1572872 | tf_op jit(solution)/shard_map/ppermute | solution.py:475
  81.6 11.3 %collective-permute-start.29 = (bf16[512,256]{1,0:T(8,128)(2,1)}, bf16[512,256]{1,0:T(8,128)(2,1)S(1)}, u32[]{:S(2)}, u32[]{:S(2)}) collective-permute-start(bf16[512,256]{1,0:T(8,128)(2,1)} %get-tuple-element.90), channel_id=1, source_target_pairs={{0,4},{1,5},{2,6},{3,7},{4,0},{5,1},{6,2},{7,3},{8,12},{9,13},{10,... | collective-permute-start | bytes 786440 | tf_op jit(solution)/shard_map/ppermute | solution.py:363
  82.1 11.3 %collective-permute-start.30 = (bf16[512,256]{1,0:T(8,128)(2,1)}, bf16[512,256]{1,0:T(8,128)(2,1)S(1)}, u32[]{:S(2)}, u32[]{:S(2)}) collective-permute-start(bf16[512,256]{1,0:T(8,128)(2,1)} %get-tuple-element.93), channel_id=1, source_target_pairs={{0,2},{1,3},{2,0},{3,1},{4,6},{5,7},{6,4},{7,5},{8,10},{9,11},{10,... | collective-permute-start | bytes 786440 | tf_op jit(solution)/shard_map/ppermute | solution.py:363
  83.1 11.6 %collective-permute-start.33 = (bf16[512,256]{1,0:T(8,128)(2,1)}, bf16[512,256]{1,0:T(8,128)(2,1)S(1)}, u32[]{:S(2)}, u32[]{:S(2)}) collective-permute-start(bf16[512,256]{1,0:T(8,128)(2,1)} %get-tuple-element.100), channel_id=1, source_target_pairs={{0,3},{1,2},{2,1},{3,0},{4,7},{5,6},{6,5},{7,4},{8,11},{9,10},{10,... | collective-permute-start | bytes 786440 | tf_op jit(solution)/shard_map/ppermute | solution.py:516
  90.2 9.7 %collective-permute-start.31 = (bf16[1024,256]{1,0:T(8,128)(2,1)S(1)}, bf16[1024,256]{1,0:T(8,128)(2,1)S(1)}, u32[]{:S(2)}, u32[]{:S(2)}) collective-permute-start(bf16[1024,256]{1,0:T(8,128)(2,1)S(1)} %pad_maximum_fusion.7), channel_id=1, source_target_pairs={{0,1},{1,0},{2,3},{3,2},{4,5},{5,4},{6,7},{7,6},{8,9},{9,8},{10,11... | collective-permute-start | bytes 1572872 | tf_op jit(solution)/shard_map/ppermute | solution.py:360
  91.4 8.3 %collective-permute-start.32 = (bf16[512,256]{1,0:T(8,128)(2,1)S(1)}, bf16[512,256]{1,0:T(8,128)(2,1)S(1)}, u32[]{:S(2)}, u32[]{:S(2)}) collective-permute-start(bf16[512,256]{1,0:T(8,128)(2,1)S(1)} %copy-done.31), channel_id=1, source_target_pairs={{0,5},{1,4},{2,7},{3,6},{4,1},{5,0},{6,3},{7,2},{8,13},{9,12},{10,... | collective-permute-start | bytes 786440 | tf_op jit(solution)/shard_map/ppermute | solution.py:516
  92.9 57.4 %collective-permute-start.23 = (bf16[256,2048]{1,0:T(8,128)(2,1)S(1)}, bf16[256,2048]{1,0:T(8,128)(2,1)S(1)}, u32[]{:S(2)}, u32[]{:S(2)}) collective-permute-start(bf16[256,2048]{1,0:T(8,128)(2,1)S(1)} %copy-done.14), channel_id=1, source_target_pairs={{0,1},{1,0},{2,3},{3,2},{4,5},{5,4},{6,7},{7,6},{8,9},{9,8},{10,11... | collective-permute-start | bytes 3145736 | tf_op jit(solution)/shard_map/ppermute | solution.py:360
  93.4 24.4 %collective-permute-start.26 = (bf16[2,2,256,256]{3,2,1,0:T(8,128)(2,1)S(1)}, bf16[2,2,256,256]{3,2,1,0:T(8,128)(2,1)S(1)}, u32[]{:S(2)}, u32[]{:S(2)}) collective-permute-start(bf16[2,2,256,256]{3,2,1,0:T(8,128)(2,1)S(1)} %pad_maximum_fusion.6), channel_id=1, source_target_pairs={{8,0},{16,8},{24,16},{9,1},{17,9},{25,17},{10,2},{18,10},{26,18},{... | collective-permute-start | bytes 1572872 | tf_op jit(solution)/shard_map/ppermute | solution.py:475
  94.7 24.5 %collective-permute-start.24 = (bf16[256,1024]{1,0:T(8,128)(2,1)S(1)}, bf16[256,1024]{1,0:T(8,128)(2,1)S(1)}, u32[]{:S(2)}, u32[]{:S(2)}) collective-permute-start(bf16[256,1024]{1,0:T(8,128)(2,1)S(1)} %copy-done.17), channel_id=1, source_target_pairs={{0,1},{1,0},{2,3},{3,2},{4,5},{5,4},{6,7},{7,6},{8,9},{9,8},{10,11... | collective-permute-start | bytes 1572872 | tf_op jit(solution)/shard_map/ppermute | solution.py:360
  100.1 19.2 %copy-start.4 = (bf16[256,1024]{1,0:T(8,128)(2,1)S(1)}, bf16[256,1024]{1,0:T(8,128)(2,1)}, u32[]{:S(2)}) copy-start(bf16[256,1024]{1,0:T(8,128)(2,1)} %get-tuple-element.86) | copy-start | bytes 1572868
  100.2 20.4 %collective-permute-start.34 = (bf16[512,256]{1,0:T(8,128)(2,1)S(1)}, bf16[512,256]{1,0:T(8,128)(2,1)S(1)}, u32[]{:S(2)}, u32[]{:S(2)}) collective-permute-start(bf16[512,256]{1,0:T(8,128)(2,1)S(1)} %get-tuple-element.114), channel_id=1, source_target_pairs={{24,16},{25,17},{26,18},{27,19},{28,20},{29,21},{30,22},{31,23}} | collective-permute-start | bytes 786440 | tf_op jit(solution)/shard_map/ppermute | solution.py:451
  101.0 19.6 %collective-permute-start.35 = (bf16[512,256]{1,0:T(8,128)(2,1)S(1)}, bf16[512,256]{1,0:T(8,128)(2,1)S(1)}, u32[]{:S(2)}, u32[]{:S(2)}) collective-permute-start(bf16[512,256]{1,0:T(8,128)(2,1)S(1)} %get-tuple-element.113), channel_id=1, source_target_pairs={{0,8},{1,9},{2,10},{3,11},{4,12},{5,13},{6,14},{7,15}} | collective-permute-start | bytes 786440 | tf_op jit(solution)/shard_map/ppermute | solution.py:451
  117.9 15.0 %collective-permute-start.27 = (bf16[1,2,256,256]{3,2,1,0:T(8,128)(2,1)S(1)}, bf16[1,2,256,256]{3,2,1,0:T(8,128)(2,1)S(1)}, u32[]{:S(2)}, u32[]{:S(2)}) collective-permute-start(bf16[1,2,256,256]{3,2,1,0:T(8,128)(2,1)S(1)} %get-tuple-element.124), channel_id=1, source_target_pairs={{8,0},{16,8},{24,16},{9,1},{17,9},{25,17},{10,2},{18,10},{26,18},{... | collective-permute-start | bytes 786440 | tf_op jit(solution)/shard_map/ppermute | solution.py:475
  119.2 13.7 %collective-permute-start.28 = (bf16[2,256,256]{2,1,0:T(8,128)(2,1)S(1)}, bf16[2,256,256]{2,1,0:T(8,128)(2,1)S(1)}, u32[]{:S(2)}, u32[]{:S(2)}) collective-permute-start(bf16[2,256,256]{2,1,0:T(8,128)(2,1)S(1)} %get-tuple-element.125), channel_id=1, source_target_pairs={{0,1},{1,0},{2,3},{3,2},{4,5},{5,4},{6,7},{7,6},{8,9},{9,8},{10,11... | collective-permute-start | bytes 786440 | tf_op jit(solution)/shard_map/ppermute | solution.py:360
  120.8 13.1 %collective-permute-start.36 = (bf16[512,256]{1,0:T(8,128)(2,1)S(1)}, bf16[512,256]{1,0:T(8,128)(2,1)S(1)}, u32[]{:S(2)}, u32[]{:S(2)}) collective-permute-start(bf16[512,256]{1,0:T(8,128)(2,1)S(1)} %get-tuple-element.112), channel_id=1, source_target_pairs={{16,8},{24,16},{17,9},{25,17},{18,10},{26,18},{19,11},{27,19},{20,... | collective-permute-start | bytes 786440 | tf_op jit(solution)/shard_map/ppermute | solution.py:451
  121.5 28.8 %copy-start = (f32[256,2048]{1,0:T(8,128)S(1)}, f32[256,2048]{1,0:T(8,128)}, u32[]{:S(2)}) copy-start(f32[256,2048]{1,0:T(8,128)} %get-tuple-element.84) | copy-start | bytes 6291460
  121.5 16.6 %collective-permute-start.37 = (bf16[512,256]{1,0:T(8,128)(2,1)S(1)}, bf16[512,256]{1,0:T(8,128)(2,1)S(1)}, u32[]{:S(2)}, u32[]{:S(2)}) collective-permute-start(bf16[512,256]{1,0:T(8,128)(2,1)S(1)} %get-tuple-element.111), channel_id=1, source_target_pairs={{0,8},{8,16},{1,9},{9,17},{2,10},{10,18},{3,11},{11,19},{4,12},{12... | collective-permute-start | bytes 786440 | tf_op jit(solution)/shard_map/ppermute | solution.py:451
  138.2 14.7 %collective-permute-start.38 = (bf16[512,256]{1,0:T(8,128)(2,1)S(1)}, bf16[512,256]{1,0:T(8,128)(2,1)S(1)}, u32[]{:S(2)}, u32[]{:S(2)}) collective-permute-start(bf16[512,256]{1,0:T(8,128)(2,1)S(1)} %get-tuple-element.110), channel_id=1, source_target_pairs={{8,0},{16,8},{24,16},{9,1},{17,9},{25,17},{10,2},{18,10},{26,18},{... | collective-permute-start | bytes 786440 | tf_op jit(solution)/shard_map/ppermute | solution.py:451
  139.5 14.6 %collective-permute-start.39 = (bf16[512,256]{1,0:T(8,128)(2,1)S(1)}, bf16[512,256]{1,0:T(8,128)(2,1)S(1)}, u32[]{:S(2)}, u32[]{:S(2)}) collective-permute-start(bf16[512,256]{1,0:T(8,128)(2,1)S(1)} %get-tuple-element.109), channel_id=1, source_target_pairs={{0,8},{8,16},{16,24},{1,9},{9,17},{17,25},{2,10},{10,18},{18,26},{... | collective-permute-start | bytes 786440 | tf_op jit(solution)/shard_map/ppermute | solution.py:451
  (26 other events, 118.5 us)
